TPU v7x, 32 devices: a whole 2x2x4 slice. The times are simulated.
32 devices in a mesh: page: 8 (over z, x), feat: 4 (over y, core).
Axes of the slice: x: 2, y: 2, z: 4, core: 2. Of those that a mesh axis runs over, the one named last changes fastest.
Arguments:
- queries: bfloat16 [64, 4096], P('page', 'feat')
- fresh_token_keys: bfloat16 [64, 2048], P('page', 'feat')
- fresh_token_values: bfloat16 [64, 2048], P('page', 'feat'), may hold values from -6 to 6
- paged_keys: bfloat16 [128, 256, 2048], P('page', None, 'feat'), may hold values from -6 to 6
- paged_values: bfloat16 [128, 256, 2048], P('page', None, 'feat'), may hold values from -6 to 6
- block_tables: int32 [64, 8], replicated, may hold values from -1 to 127, as said below
- parents: int32 [64], replicated, may hold values from 0 to 63, as said below
- prompt_lengths: int32 [8], replicated, may hold values from 1 to 2047, as said below
- stream: bfloat16 [64, 4608], P(('page', 'feat'))
- output_matrix: bfloat16 [4608, 4096], P(None, 'feat')
- attention_gain: bfloat16 [4608], replicated, may hold values from 0.5 to 1.5
- feedforward_gain: bfloat16 [4608], replicated, may hold values from 0.5 to 1.5
- gate_matrix: bfloat16 [36864, 4608], P(('page', 'feat')), may hold values from -0.09375 to 0.09375
- linear_matrix: bfloat16 [36864, 4608], P(('page', 'feat')), may hold values from -0.09375 to 0.09375
- down_matrix: bfloat16 [36864, 4608], P(('page', 'feat'))
- closing_gain: bfloat16 [4608], replicated, may hold values from 0.5 to 1.5
Outputs:
- layer_output: bfloat16 [64, 4608], P(('page', 'feat'))
Inputs may be any that keep to these rules, and one draw needn't show every extreme that they name: `block_tables`: row r's table lists the page slots of its blocks in order; entries from ceil(prompt_lengths[r // 8] / 256) on are -1. Rows of one prompt list the same slots for all but their last listed block, which is each row's own. A slot is listed by the rows of one prompt only, and at most once in a row. `prompt_lengths`: the new token of each prompt's rows stands at this position. `parents`: the parent of row r is a row of the same prompt, from 8 * (r // 8) to that plus 8 - 1.
All inputs are finite; a program needn't handle non-finite values.
Results may differ from a plain program's by a relative error of at most 0.0095.
Values may be sent and summed in bfloat16 or wider, within the bound.
A program may use at most 128 MiB of HBM per device.

v0:
```python
import math

import jax
import jax.numpy as jnp
from jax import lax
from jax.sharding import PartitionSpec as P

HEAD_DIM_SIZE = 128
QSCALAR = 144
SOFTCAP = 50
BEAMS = 8


norm_eps = 1e-06


def capped(scores):
    return SOFTCAP * jnp.tanh(scores / SOFTCAP)


def normalize(values, gain_row):
    mean_square = jnp.mean(values * values, axis=1, keepdims=True)
    return values * lax.rsqrt(mean_square + norm_eps) * gain_row.astype(jnp.float32)[None, :]


def activate(segment, gate_matrix, linear_matrix):
    gate_sums = lax.dot_general(
        segment, gate_matrix, (((1,), (1,)), ((), ())), preferred_element_type=jnp.float32
    )
    lift_sums = lax.dot_general(
        segment, linear_matrix, (((1,), (1,)), ((), ())), preferred_element_type=jnp.float32
    )
    return (jax.nn.gelu(gate_sums, approximate=True) * lift_sums).astype(jnp.bfloat16)


def per_device(
    queries,
    fresh_token_keys,
    fresh_token_values,
    paged_keys,
    paged_values,
    block_tables,
    parents,
    prompt_lengths,
    stream,
    output_matrix,
    attention_gain,
    feedforward_gain,
    gate_matrix,
    linear_matrix,
    down_matrix,
    closing_gain,
):
    home_rows = queries.shape[0]
    slot_count = paged_keys.shape[0]
    page_len = paged_keys.shape[1]
    kv_heads = paged_keys.shape[2] // HEAD_DIM_SIZE
    query_groups = queries.shape[1] // HEAD_DIM_SIZE // kv_heads
    root_scale = math.sqrt(QSCALAR)
    all_queries = lax.all_gather(queries, "page", axis=0, tiled=True)
    row_count = all_queries.shape[0]
    row_tables = jnp.take(block_tables, parents, axis=0)
    slot_ids = lax.axis_index("page") * slot_count + jnp.arange(slot_count, dtype=jnp.int32)
    matches = row_tables[None, :, :] == slot_ids[:, None, None]
    in_use = jnp.any(matches, axis=2)
    block_index = jnp.arange(row_tables.shape[1], dtype=jnp.int32)
    block_pos = jnp.sum(jnp.where(matches, block_index[None, None, :], 0), axis=2)
    row_ids = jnp.arange(row_count, dtype=jnp.int32)
    owner_prompt = jnp.max(jnp.where(in_use, (row_ids // BEAMS)[None, :], -1), axis=1)
    prompt_ids = jnp.maximum(owner_prompt, 0)
    beam_rows = prompt_ids[:, None] * BEAMS + jnp.arange(BEAMS, dtype=jnp.int32)[None, :]
    row_in_use = jnp.take_along_axis(in_use, beam_rows, axis=1)
    row_block = jnp.take_along_axis(block_pos, beam_rows, axis=1)
    limits = jnp.take(prompt_lengths, prompt_ids)
    positions = (
        row_block[:, :, None] * page_len + jnp.arange(page_len, dtype=jnp.int32)[None, None, :]
    )
    visible = jnp.logical_and(row_in_use[:, :, None], positions < limits[:, None, None])
    slot_queries = jnp.take(all_queries, beam_rows.reshape(-1), axis=0).reshape(
        slot_count, BEAMS, kv_heads, query_groups, HEAD_DIM_SIZE
    )
    page_keys = paged_keys.reshape(slot_count, page_len, kv_heads, HEAD_DIM_SIZE)
    page_values = paged_values.reshape(slot_count, page_len, kv_heads, HEAD_DIM_SIZE)
    raw_scores = jnp.einsum(
        "sbkgd,stkd->sbkgt", slot_queries, page_keys, preferred_element_type=jnp.float32
    )
    weights = jnp.where(
        visible[:, :, None, None, :], jnp.exp(capped(raw_scores / root_scale)), jnp.float32(0.0)
    )
    slot_totals = jnp.sum(weights, axis=4)
    slot_numerators = jnp.einsum(
        "sbkgt,stkd->sbkgd",
        weights.astype(jnp.bfloat16),
        page_values,
        preferred_element_type=jnp.float32,
    )
    selector = (beam_rows[:, :, None] == row_ids[None, None, :]).astype(jnp.float32)
    numerator_rows = jnp.einsum(
        "avz,avo->zo",
        selector,
        slot_numerators.reshape(slot_count, BEAMS, -1),
        precision=lax.Precision.HIGHEST,
    )
    total_rows = jnp.einsum(
        "avz,avo->zo",
        selector,
        slot_totals.reshape(slot_count, BEAMS, -1),
        precision=lax.Precision.HIGHEST,
    )
    home_numerators, home_totals = (
        lax.psum_scatter(numerator_rows, "page", scatter_dimension=0, tiled=True),
        lax.psum_scatter(total_rows, "page", scatter_dimension=0, tiled=True),
    )
    own_queries = queries.reshape(home_rows, kv_heads, query_groups, HEAD_DIM_SIZE)
    own_keys = fresh_token_keys.reshape(home_rows, kv_heads, HEAD_DIM_SIZE)
    own_values = fresh_token_values.reshape(home_rows, kv_heads, HEAD_DIM_SIZE)
    self_weight = jnp.exp(
        capped(
            jnp.einsum("rkgd,rkd->rkg", own_queries, own_keys, preferred_element_type=jnp.float32)
            / root_scale
        )
    )
    totals = home_totals.reshape(home_rows, kv_heads, query_groups) + self_weight
    self_term = jnp.einsum(
        "rkg,rkd->rkgd",
        self_weight.astype(jnp.bfloat16),
        own_values,
        preferred_element_type=jnp.float32,
    )
    numerators = (
        home_numerators.reshape(home_rows, kv_heads, query_groups, HEAD_DIM_SIZE) + self_term
    )
    attention = (numerators / totals[:, :, :, None]).reshape(home_rows, -1).astype(jnp.bfloat16)
    head_terms = lax.dot_general(
        attention, output_matrix, (((1,), (1,)), ((), ())), preferred_element_type=jnp.float32
    )
    projected = lax.psum_scatter(head_terms, "feat", scatter_dimension=0, tiled=True)
    residual = stream.astype(jnp.float32) + normalize(projected, attention_gain)
    normed = normalize(residual, feedforward_gain).astype(jnp.bfloat16)
    page_count = lax.axis_size("page")
    feat_count = lax.axis_size("feat")
    lot_rows = lax.all_gather(normed, "page", axis=0, tiled=True).reshape(
        page_count, 1, normed.shape[0], normed.shape[1]
    )
    segment = lax.all_gather(lot_rows, "feat", axis=1, tiled=True)
    flattened = segment.reshape(-1, segment.shape[3])
    hidden = (
        activate(flattened, gate_matrix, linear_matrix)
        .reshape(segment.shape[0], segment.shape[1], segment.shape[2], -1)
        .reshape(-1, gate_matrix.shape[0])
    )
    term_rows = jnp.dot(hidden, down_matrix, preferred_element_type=jnp.float32).reshape(
        page_count, feat_count, normed.shape[0], -1
    )
    partly = lax.psum_scatter(term_rows, "feat", scatter_dimension=1, tiled=True)
    feedforward = lax.psum_scatter(partly, "page", scatter_dimension=0, tiled=True).reshape(
        normed.shape[0], -1
    )
    return (residual + normalize(feedforward, closing_gain)).astype(jnp.bfloat16)


def solution(mesh):
    placed = (
        P("page", "feat"),
        P("page", "feat"),
        P("page", "feat"),
        P("page", None, "feat"),
        P("page", None, "feat"),
        P(),
        P(),
        P(),
        P(("page", "feat"), None),
        P(None, "feat"),
        P(),
        P(),
        P(("page", "feat"), None),
        P(("page", "feat"), None),
        P(("page", "feat"), None),
        P(),
    )
    return jax.shard_map(
        per_device, mesh=mesh, in_specs=placed, out_specs=P(("page", "feat"), None), check_vma=False
    )
```

profile of v0, /device:TPU:0, one launch (start us, length us, event | category | flops | bytes accessed | tf_op | source)
XLA Modules:
  0.0 343.9 jit_solution(5222165970779979272)
XLA Ops:
  9.8 1.3 gather_fusion.1
  11.3 1.5 gather_fusion.3
  12.8 1.3 gather_fusion.4
  14.6 32.3 %all_gather.9 = bf16[64,1024]{1,0:T(8,128)(2,1)S(1)} all-gather(bf16[8,1024]{1,0:T(8,128)(2,1)S(1)} %copy-done.2), channel_id=1, replica_groups=mesh['page'=8,'feat'=4] {'page'}, dimensions={0}, use_global_device_ids=true | all-gather | bytes 147456 | tf_op jit(solution)/shard_map/all_gather | solution.py:60
  46.9 6.9 %reshape.299 = bf16[16,256,4,128]{3,2,1,0:T(4,128)(2,1)} reshape(bf16[16,256,512]{2,1,0:T(8,128)(2,1)} %param.19) | data formatting | bytes 8388608 | tf_op jit(solution)/shard_map/reshape | solution.py:82
  53.9 6.9 %reshape.300 = bf16[16,256,4,128]{3,2,1,0:T(4,128)(2,1)} reshape(bf16[16,256,512]{2,1,0:T(8,128)(2,1)} %param.20) | data formatting | bytes 8388608 | tf_op jit(solution)/shard_map/reshape | solution.py:83
  61.8 3.6 %fusion.64 = (f32[16,8,4,2]{1,3,2,0:T(2,128)S(1)}, bf16[16,8,4,2,256]{4,1,3,2,0:T(8,128)(2,1)S(1)}) fusion(bf16[16,256,4,128,1]{3,2,1,0,4:T(4,128)(2,1)} %bitcast.61, bf16[16,8,4,2,128]{4,1,3,2,0:T(8,128)(2,1)S(1)} %bitcast.64, pred[16,8]{1,0:T(8,128)(4,1)S(1)} %get-tuple-element.9, pred[16,8,256]{2,1,0:T(8,128)(4,1)S(1)} %fusion.41), kind=kOutput, calls=%fused_computation.100 | convolution fusion | flops 68549632 | bytes 5017728 | tf_op jit(solution)/shard_map/sbkgd,stkd->sbkgt/dot_general | solution.py:84
  65.4 2.9 fusion
  68.3 1.4 convolution_bitcast_fusion
  70.2 37.1 %all-reduce = f32[64,8]{1,0:T(8,128)S(1)} all-reduce(f32[64,8]{1,0:T(8,128)S(1)} %convolution_bitcast_fusion.1), channel_id=3, replica_groups=mesh['page'=8,'feat'=4] {'page'}, use_global_device_ids=true, to_apply=%region_5.6.clone | all-reduce | flops 512 | bytes 4096
  108.9 23.5 %reduce-scatter.3.cloned.1.call-done = f32[8,1024]{1,0:T(8,128)} async-done(((f32[64,1024]{1,0:T(8,128)}), f32[8,1024]{1,0:T(8,128)}) %reduce-scatter.3.cloned.1.call-update) | async-done | bytes 32784 | tf_op jit(solution)/shard_map/reduce_scatter | solution.py:111
  133.3 6.9 %fusion.65 = f32[8,4608]{1,0:T(8,128)} fusion(bf16[8,1024]{1,0:T(8,128)(2,1)S(1)} %bitcast.65, bf16[4608,1024]{1,0:T(8,128)(2,1)} %param.25), kind=kOutput, calls=%fused_computation.101 | convolution fusion | flops 75497472 | bytes 9601024 | tf_op jit(solution)/shard_map/dot_general | solution.py:134
  141.5 28.6 %all-reduce.6.cloned.1.call-done = f32[8,4608]{1,0:T(8,128)} async-done(((f32[8,4608]{1,0:T(8,128)}), f32[8,4608]{1,0:T(8,128)}) %all-reduce.6.cloned.1.call-update) | async-done | bytes 147472
  171.2 1.1 multiply_reduce_fusion.1
  172.4 30.7 %all-gather = bf16[8,2,4608]{2,1,0:T(2,128)(2,1)S(1)} all-gather(bf16[1,2,4608]{2,1,0:T(2,128)(2,1)S(1)} %fusion.47), channel_id=1, replica_groups=mesh['page'=8,'feat'=4] {'page'}, dimensions={0}, use_global_device_ids=true | all-gather | bytes 165888 | tf_op jit(solution)/shard_map/all_gather | solution.py:142
  203.1 7.5 %all_gather.11 = bf16[8,4,2,4608]{3,0,2,1:T(8,128)(2,1)S(1)} all-gather(bf16[8,1,2,4608]{3,0,2,1:T(8,128)(2,1)S(1)} %copy.48), channel_id=1, replica_groups=mesh['page'=8,'feat'=4] {'feat'}, dimensions={1}, use_global_device_ids=true | all-gather | bytes 737280 | tf_op jit(solution)/shard_map/all_gather | solution.py:145
  211.3 7.3 %fusion.66 = f32[64,1152]{1,0:T(8,128)S(1)} fusion(bf16[64,4608]{1,0:T(8,128)(2,1)S(1)} %reshape.309, bf16[1152,4608]{1,0:T(8,128)(2,1)} %param.28), kind=kOutput, calls=%fused_computation.102 | convolution fusion | flops 679477248 | bytes 11501568 | tf_op jit(solution)/shard_map/dot_general | solution.py:27
  218.7 12.6 %fusion.23 = f32[64,4608]{1,0:T(8,128)S(1)} fusion(bf16[1152,4608]{1,0:T(8,128)(2,1)} %param.30, bf16[64,4608]{1,0:T(8,128)(2,1)S(1)} %reshape.309, bf16[1152,4608]{1,0:T(8,128)(2,1)} %param.29, f32[64,1152]{1,0:T(8,128)S(1)} %fusion.66), kind=kOutput, calls=%fused_computation.19 | convolution fusion | flops 1359691776 | bytes 23298048 | tf_op jit(solution)/shard_map/dot_general | solution.py:152
  231.9 1.7 copy.50
  233.7 25.9 %reduce-scatter.5.cloned.1.call-done = f32[8,1,2,4608]{3,0,2,1:T(8,128)} async-done(((f32[8,4,2,4608]{3,0,2,1:T(8,128)}), f32[8,1,2,4608]{3,0,2,1:T(8,128)}) %reduce-scatter.5.cloned.1.call-update) | async-done | bytes 294928 | tf_op jit(solution)/shard_map/reduce_scatter | solution.py:155
  259.6 1.9 copy.51
  261.5 72.2 %all-reduce.8.cloned.1.call-done = f32[8,1,2,4608]{3,2,1,0:T(2,128)} async-done(((f32[8,1,2,4608]{3,2,1,0:T(2,128)}), f32[8,1,2,4608]{3,2,1,0:T(2,128)}) %all-reduce.8.cloned.1.call-update) | async-done | bytes 294928
  333.7 1.5 multiply_reduce_fusion
  335.2 2.1 add_convert_fusion
  (76 shorter events, 10.6 us)
Async XLA Ops:
  6.5 102.0 %copy-start = (bf16[8,512]{1,0:T(8,128)(2,1)S(1)}, bf16[8,512]{1,0:T(8,128)(2,1)}, u32[]{:S(2)}) copy-start(bf16[8,512]{1,0:T(8,128)(2,1)} %param.17) | copy-start | bytes 24580
  6.5 8.1 %copy-start.2 = (bf16[8,1024]{1,0:T(8,128)(2,1)S(1)}, bf16[8,1024]{1,0:T(8,128)(2,1)}, u32[]{:S(2)}) copy-start(bf16[8,1024]{1,0:T(8,128)(2,1)} %param.16) | copy-start | bytes 49156
  6.5 125.9 %reduce-scatter.3.cloned.1.call-start = ((), (), s32[]{:S(2)}) async-start(), calls=%async_computation.2 | async-start | bytes 294912 | tf_op jit(solution)/shard_map/reduce_scatter | solution.py:111
  60.8 46.5 %copy-start.8 = (u32[32]{0:T(128)S(1)}, u32[32]{0:T(128)}, u32[]{:S(2)}) copy-start(u32[32]{0:T(128)} %constant.161) | copy-start | bytes 388
  60.8 48.1 %copy-start.6 = (bf16[8,512]{1,0:T(8,128)(2,1)S(1)}, bf16[8,512]{1,0:T(8,128)(2,1)}, u32[]{:S(2)}) copy-start(bf16[8,512]{1,0:T(8,128)(2,1)} %param.18) | copy-start | bytes 24580
  65.4 74.8 %copy-start.7 = (u32[32]{0:T(128)S(1)}, u32[32]{0:T(128)}, u32[]{:S(2)}) copy-start(u32[32]{0:T(128)} %constant.165) | copy-start | bytes 388
  65.4 75.4 %copy-start.3 = (bf16[4608]{0:T(1024)(128)(2,1)S(1)}, bf16[4608]{0:T(1024)(128)(2,1)}, u32[]{:S(2)}) copy-start(bf16[4608]{0:T(1024)(128)(2,1)} %param.26) | copy-start | bytes 27652
  65.4 75.4 %copy-start.4 = (bf16[4608]{0:T(1024)(128)(2,1)S(1)}, bf16[4608]{0:T(1024)(128)(2,1)}, u32[]{:S(2)}) copy-start(bf16[4608]{0:T(1024)(128)(2,1)} %param.27) | copy-start | bytes 27652
  65.4 105.8 %copy-start.1 = (bf16[2,4608]{1,0:T(2,128)(2,1)S(1)}, bf16[2,4608]{1,0:T(2,128)(2,1)}, u32[]{:S(2)}) copy-start(bf16[2,4608]{1,0:T(2,128)(2,1)} %param.24) | copy-start | bytes 55300
  69.7 100.4 %all-reduce.6.cloned.1.call-start = ((), (), s32[]{:S(2)}) async-start(), calls=%async_computation.4 | async-start | bytes 294912
  140.2 119.4 %reduce-scatter.5.cloned.1.call-start = ((), (), s32[]{:S(2)}) async-start(), calls=%async_computation.3 | async-start | bytes 1474560 | tf_op jit(solution)/shard_map/reduce_scatter | solution.py:155
  218.7 42.8 %copy-start.5 = (bf16[4608]{0:T(1024)(128)(2,1)S(1)}, bf16[4608]{0:T(1024)(128)(2,1)}, u32[]{:S(2)}) copy-start(bf16[4608]{0:T(1024)(128)(2,1)} %param.31) | copy-start | bytes 27652
  233.7 100.0 %all-reduce.8.cloned.1.call-start = ((), (), s32[]{:S(2)}) async-start(), calls=%async_computation.5 | async-start | bytes 589824
Sparse Core Ops, SparseCore 0:
  69.8 62.5 reduce-scatter.2
  140.3 29.7 all-reduce.5
  233.8 25.7 reduce-scatter.4
  262.8 70.8 all-reduce.7
where the time goes:
time: 345 us; the launch traced here: 344 us
  waiting for transfers between devices  150 us (43%)
  blocking collectives  108 us (31%)
  matrix products  35.1 us (10%)
  local copies, waits for them, and re-layouts  27.2 us (8%)
  between operations  14.7 us (4%)
  other arithmetic  8.98 us (3%)
    unnamed x6, waiting for transfers between devices  101 us
    unnamed x1, blocking collectives  37.1 us
    all_gather x1, blocking collectives, per_device(): all_queries = lax.all_gather(queries, 'page', axis=0, tiled=True)  32.3 us
    all_gather x1, blocking collectives, per_device(): lax.all_gather(normed, 'page', axis=0, tiled=True)  30.7 us
    reduce_scatter x1, waiting for transfers between devices, per_device(): lax.psum_scatter(term_rows, 'feat', scatter_dimension=1, tiled=True)  25.9 us
    reduce_scatter x1, waiting for transfers between devices, per_device(): lax.psum_scatter(numerator_rows, 'page', scatter_dimension=0, tiled=True)  23.5 us
    dot_general x1, matrix products, per_device(): jnp.dot(hidden, down_matrix, preferred_element_type=jnp.float32)  12.6 us
    all_gather x1, blocking collectives, per_device(): segment = lax.all_gather(lot_rows, 'feat', axis=1, tiled=True)  7.52 us
  transfers between devices with their start and end apart: 4, of which 4 were waited for; matrix products, arithmetic and copies ran while one was open for 1% of the time, Pallas kernels for 0%

commit v1 on v0

v1 whole, which is shorter than its diff:
```python
import functools
import math

import jax
import jax.numpy as jnp
from jax import lax
from jax.experimental import pallas as pl
from jax.experimental.pallas import tpu as pltpu
from jax.sharding import PartitionSpec as P

HEAD = 128
QSCALAR = 144
SOFTCAP = 50
BEAMS = 8
EPS = 1e-06

F32 = jnp.float32
BF16 = jnp.bfloat16
MESH = pl.DeviceIdType.MESH
NT = (((1,), (1,)), ((), ()))
NN = (((1,), (0,)), ((), ()))


def capped_exp(raw):
    return jnp.exp(SOFTCAP * jnp.tanh(raw * (1.0 / (math.sqrt(QSCALAR) * SOFTCAP))))


def mm(a, b, dims):
    return lax.dot_general(a, b, dims, preferred_element_type=F32)


def layer_kernel(
    n_page, n_feat, width, depth,
    q_ref, fk_ref, fv_ref, by_col_ref, by_row_ref, stream_ref, gains_ref,
    keys_hbm, values_hbm, wo_hbm, gate_hbm, lift_hbm, down_hbm,
    out_ref,
    kbuf, vbuf, wo, gate, lift, down,
    allq, qs, nvs, snum, stot, nsend, nrecv, att, strm, prj, res,
    xg, xs, gacc, uacc, hid, core_s, core_r, y_s, y_r, psend, precv, fsend, frecv,
    kv_sem, w_sem,
    q_ss, q_rs, n_ss, n_rs, st_ss, st_rs, pj_ss, pj_rs, ag_ss, ag_rs,
    xy_ss, xc_ss, x_rs, c_ss, c_rs, y_ss, y_rs, p_ss, p_rs, f_ss, f_rs,
):
    page = lax.axis_index("page")
    feat = lax.axis_index("feat")
    ny = n_feat // 2
    yy, cc = feat // 2, feat % 2
    mate = yy * 2 + (1 - cc)
    slots, page_len, kvw = kbuf.shape
    kv_heads = kvw // HEAD
    heads = q_ref.shape[1] // HEAD
    groups = heads // kv_heads
    rows = n_page * BEAMS
    home = stream_ref.shape[0]
    hw = heads * HEAD

    def cut(c):
        return min(width, depth - c * width)

    local = [
        pltpu.make_async_copy(keys_hbm, kbuf, kv_sem.at[0]),
        pltpu.make_async_copy(values_hbm, vbuf, kv_sem.at[1]),
    ]
    w_copies = [[], [], [], []]
    for c in range(n_feat):
        part = pl.ds(c * width, cut(c))
        have = pl.ds(0, cut(c))
        w_copies[0].append(pltpu.make_async_copy(wo_hbm.at[part, :], wo.at[c, have, :], w_sem.at[0, c]))
        w_copies[1].append(pltpu.make_async_copy(gate_hbm.at[:, part], gate.at[c, :, have], w_sem.at[1, c]))
        w_copies[2].append(pltpu.make_async_copy(lift_hbm.at[:, part], lift.at[c, :, have], w_sem.at[2, c]))
        w_copies[3].append(pltpu.make_async_copy(down_hbm.at[:, part], down.at[c, :, have], w_sem.at[3, c]))
        if cut(c) < width:
            rest = width - cut(c)
            wo[c, cut(c):, :] = jnp.zeros((rest, wo.shape[2]), BF16)
            gate[c, :, cut(c):] = jnp.zeros((gate.shape[1], rest), BF16)
            lift[c, :, cut(c):] = jnp.zeros((gate.shape[1], rest), BF16)
            down[c, :, cut(c):] = jnp.zeros((gate.shape[1], rest), BF16)
    for copy in local:
        copy.start()
    for kind in w_copies:
        for copy in kind:
            copy.start()

    barrier = pltpu.get_barrier_semaphore()

    def greet_page(d, _):
        pl.semaphore_signal(barrier, inc=1, device_id=((page + d) % n_page, feat), device_id_type=MESH)
        return 0

    def greet_feat(d, _):
        pl.semaphore_signal(barrier, inc=1, device_id=(page, (feat + d) % n_feat), device_id_type=MESH)
        return 0

    lax.fori_loop(1, n_page, greet_page, 0)
    lax.fori_loop(1, n_feat, greet_feat, 0)

    allq[page] = q_ref[...]
    sf = stream_ref[...].astype(F32)
    if strm.shape[2] > depth:
        sf = jnp.concatenate([sf, jnp.zeros((home, strm.shape[2] - depth), F32)], axis=1)
    strm[feat] = sf
    pl.semaphore_wait(barrier, n_page + n_feat - 2)

    def page_copy(src, dst, ss, rs):
        def send(d):
            peer = (page + d) % n_page
            return pltpu.make_async_remote_copy(
                src_ref=src(peer), dst_ref=dst(page), send_sem=ss.at[peer], recv_sem=rs.at[page],
                device_id=(peer, feat), device_id_type=MESH)

        def arrival(d):
            peer = (page + d) % n_page
            return pltpu.make_async_remote_copy(
                src_ref=src(peer), dst_ref=dst(peer), send_sem=ss.at[peer], recv_sem=rs.at[peer],
                device_id=(peer, feat), device_id_type=MESH)

        def start():
            lax.fori_loop(1, n_page, lambda d, z: (send(d).start(), z)[1], 0)

        def wait_recv():
            lax.fori_loop(1, n_page, lambda d, z: (arrival(d).wait_recv(), z)[1], 0)

        def wait_send():
            lax.fori_loop(1, n_page, lambda d, z: (send(d).wait_send(), z)[1], 0)

        return start, wait_recv, wait_send

    def feat_copy(src, dst, ss, rs):
        def send(d):
            peer = (feat + d) % n_feat
            return pltpu.make_async_remote_copy(
                src_ref=src(peer), dst_ref=dst(feat), send_sem=ss(peer), recv_sem=rs(feat),
                device_id=(page, peer), device_id_type=MESH)

        def arrival(d):
            peer = (feat + d) % n_feat
            return pltpu.make_async_remote_copy(
                src_ref=src(peer), dst_ref=dst(peer), send_sem=ss(peer), recv_sem=rs(peer),
                device_id=(page, peer), device_id_type=MESH)

        def start():
            lax.fori_loop(1, n_feat, lambda d, z: (send(d).start(), z)[1], 0)

        def wait_recv():
            lax.fori_loop(1, n_feat, lambda d, z: (arrival(d).wait_recv(), z)[1], 0)

        def wait_send():
            lax.fori_loop(1, n_feat, lambda d, z: (send(d).wait_send(), z)[1], 0)

        return start, wait_recv, wait_send

    q_start, q_wait, q_done = page_copy(lambda p: allq.at[page], lambda p: allq.at[p], q_ss, q_rs)
    q_start()
    st_start, st_wait, st_done = feat_copy(
        lambda p: strm.at[feat], lambda p: strm.at[p], lambda p: st_ss.at[p], lambda p: st_rs.at[p])
    st_start()

    blocks = by_col_ref.shape[0] - 1
    sb = slots * BEAMS
    down_i = lax.broadcasted_iota(jnp.int32, (sb, rows), 0)
    across = lax.broadcasted_iota(jnp.int32, (sb, rows), 1)
    seen = jnp.zeros((sb, rows), jnp.int32)
    lens = by_col_ref[blocks:blocks + 1, :]
    for b in range(blocks):
        seen += jnp.where(by_col_ref[b:b + 1, :] == page * slots + down_i // BEAMS,
                          jnp.clip(lens - b * page_len, 0, page_len), 0)
    seen = jnp.where(across % BEAMS == down_i % BEAMS, seen, 0).astype(F32)
    pick = jnp.where(seen > 0, 1.0, 0.0).astype(BF16)
    nvs[...] = jnp.broadcast_to(jnp.sum(seen, axis=1, keepdims=True), nvs.shape)

    down_t = lax.broadcasted_iota(jnp.int32, (rows, sb), 0)
    across_t = lax.broadcasted_iota(jnp.int32, (rows, sb), 1)
    seen_t = jnp.zeros((rows, sb), jnp.int32)
    lens_t = by_row_ref[:, blocks:blocks + 1]
    for b in range(blocks):
        seen_t += jnp.where(by_row_ref[:, b:b + 1] == page * slots + across_t // BEAMS,
                            jnp.clip(lens_t - b * page_len, 0, page_len), 0)
    pick_t = jnp.where(jnp.logical_and(across_t % BEAMS == down_t % BEAMS, seen_t > 0), 1.0, 0.0).astype(BF16)

    q_wait()
    q_all = allq[...].astype(F32).reshape(rows, hw).astype(BF16)
    qs[...] = mm(pick, q_all, NN)
    for copy in local:
        copy.wait()

    lane = lax.broadcasted_iota(jnp.int32, (BEAMS, HEAD), 1)
    position = lax.broadcasted_iota(jnp.int32, (groups * BEAMS, page_len), 1).astype(F32)

    def one_slot(s):
        at = pl.ds(pl.multiple_of(s * BEAMS, BEAMS), BEAMS)
        limit = jnp.concatenate([nvs[at, :]] * groups, axis=0)[:, 0:1]
        visible = position < limit
        sums = jnp.zeros((BEAMS, HEAD), F32)
        for k in range(kv_heads):
            kv = slice(k * HEAD, (k + 1) * HEAD)
            qk = jnp.concatenate(
                [qs[at, (k * groups + g) * HEAD:(k * groups + g + 1) * HEAD] for g in range(groups)], axis=0)
            raw = mm(qk.astype(BF16), kbuf[s, :, kv], NT)
            w = jnp.where(visible, capped_exp(raw), 0.0)
            tot = jnp.sum(w, axis=1, keepdims=True)
            num = mm(w.astype(BF16), vbuf[s, :, kv], NN)
            for g in range(groups):
                h = k * groups + g
                snum[at, h * HEAD:(h + 1) * HEAD] = num[g * BEAMS:(g + 1) * BEAMS]
                sums = jnp.where(lane == h, tot[g * BEAMS:(g + 1) * BEAMS], sums)
        stot[at, :] = sums

    per = 2 if slots % 2 == 0 else 1

    def some_slots(i, z):
        for u in range(per):
            one_slot(i * per + u)
        return z

    lax.fori_loop(0, slots // per, some_slots, 0)

    def to_rows(v):
        hi = v.astype(BF16)
        lo = (v - hi.astype(F32)).astype(BF16)
        return mm(pick_t, hi, NN) + mm(pick_t, lo, NN)

    tot_rows = to_rows(stot[...])
    tot_hi = tot_rows.astype(BF16)
    tot_lo = tot_rows - tot_hi.astype(F32)
    nsend[:, :, 0:hw] = to_rows(snum[...]).reshape(n_page, BEAMS, hw).astype(BF16)
    nsend[:, :, hw:hw + HEAD] = tot_hi.astype(F32).reshape(n_page, BEAMS, HEAD).astype(BF16)
    nsend[:, :, hw + HEAD:hw + 2 * HEAD] = tot_lo.reshape(n_page, BEAMS, HEAD).astype(BF16)
    nrecv[page] = nsend[page]
    n_start, n_wait, n_done = page_copy(lambda p: nsend.at[p], lambda p: nrecv.at[p], n_ss, n_rs)
    n_start()

    own_w = []
    for h in range(heads):
        k = h // groups
        qk = q_ref[:, h * HEAD:(h + 1) * HEAD].astype(F32) * fk_ref[:, k * HEAD:(k + 1) * HEAD].astype(F32)
        own_w.append(capped_exp(jnp.sum(qk, axis=1, keepdims=True)))
    n_wait()
    totals = jnp.sum(nrecv[:, :, hw:hw + HEAD].astype(F32) + nrecv[:, :, hw + HEAD:hw + 2 * HEAD].astype(F32), axis=0)
    for h in range(heads):
        k = h // groups
        hs = slice(h * HEAD, (h + 1) * HEAD)
        num = jnp.sum(nrecv[:, :, hs].astype(F32), axis=0)
        num += own_w[h].astype(BF16).astype(F32) * fv_ref[:, k * HEAD:(k + 1) * HEAD].astype(F32)
        att[:, hs] = (num / (totals[:, h:h + 1] + own_w[h])).astype(BF16)

    for copy in w_copies[0]:
        copy.wait()

    def pj(c):
        return feat_copy(lambda p: prj.at[feat, c], lambda p: prj.at[p, c],
                         lambda p: pj_ss.at[p, c], lambda p: pj_rs.at[p, c])

    def project(c, z):
        prj[feat, c] = mm(att[...], wo[c], NT).astype(BF16)
        pj(c)[0]()
        return z

    lax.fori_loop(0, n_feat, project, 0)
    st_wait()
    lax.fori_loop(0, n_feat, lambda c, z: (pj(c)[1](), z)[1], 0)

    square = jnp.zeros((BEAMS, 1), F32)
    for c in range(n_feat):
        v = jnp.sum(prj[:, c].astype(F32), axis=0)
        res[c] = v
        square += jnp.sum(v * v, axis=1, keepdims=True)
    scale = lax.rsqrt(square / depth + EPS)
    square = jnp.zeros((BEAMS, 1), F32)
    for c in range(n_feat):
        cols = slice(c * width, (c + 1) * width)
        base = jnp.concatenate([strm[g, :, cols] for g in range(n_feat)], axis=0)
        v = base + res[c] * scale * gains_ref[0, c]
        res[c] = v
        square += jnp.sum(v * v, axis=1, keepdims=True)
    scale = lax.rsqrt(square / depth + EPS)
    xg[feat, page] = (res[feat] * scale * gains_ref[1, feat]).astype(BF16)

    ag_start, ag_wait, ag_done = page_copy(
        lambda p: xg.at[feat, page], lambda p: xg.at[feat, p], ag_ss, ag_rs)
    ag_start()
    for kind in w_copies[1:3]:
        for copy in kind:
            copy.wait()

    def chunk_copy(q, peer, ss):
        return pltpu.make_async_remote_copy(
            src_ref=xg.at[q], dst_ref=xg.at[q], send_sem=ss, recv_sem=x_rs.at[q],
            device_id=(page, peer), device_id_type=MESH)

    ag_wait()
    sends = []
    for d in range(1, ny):
        sends.append(chunk_copy(feat, ((yy + d) % ny) * 2 + cc, xy_ss.at[d]))
        sends[-1].start()
    sends.append(chunk_copy(feat, mate, xc_ss.at[0]))
    sends[-1].start()
    for d in range(ny):
        for o in range(2):
            q = ((yy + ny - d) % ny) * 2 + (cc if o == 0 else 1 - cc)
            if d or o:
                chunk_copy(q, mate, xc_ss.at[d]).wait_recv()
            if d and not o:
                sends.append(chunk_copy(q, mate, xc_ss.at[d]))
                sends[-1].start()
            xs[...] = xg[q].astype(F32).reshape(rows, width).astype(BF16)
            if d or o:
                gacc[...] += mm(xs[...], gate[q], NT)
                uacc[...] += mm(xs[...], lift[q], NT)
            else:
                gacc[...] = mm(xs[...], gate[q], NT)
                uacc[...] = mm(xs[...], lift[q], NT)
    hid[...] = (jax.nn.gelu(gacc[...], approximate=True) * uacc[...]).astype(BF16)

    for copy in w_copies[3]:
        copy.wait()
    total = None
    for d in list(range(1, ny)) + [0]:
        yq = (yy + d) % ny
        core_s[d] = mm(hid[...], down[yq * 2 + (1 - cc)], NN).astype(BF16)
        over = pltpu.make_async_remote_copy(
            src_ref=core_s.at[d], dst_ref=core_r.at[d], send_sem=c_ss.at[d], recv_sem=c_rs.at[d],
            device_id=(page, mate), device_id_type=MESH)
        over.start()
        sends.append(over)
        part = mm(hid[...], down[yq * 2 + cc], NN)
        over.wait_recv()
        part = part + core_r[d].astype(F32)
        if d:
            y_s[d - 1] = part.astype(BF16)
            along = pltpu.make_async_remote_copy(
                src_ref=y_s.at[d - 1], dst_ref=y_r.at[d - 1], send_sem=y_ss.at[d - 1], recv_sem=y_rs.at[d - 1],
                device_id=(page, yq * 2 + cc), device_id_type=MESH)
            along.start()
            sends.append(along)
        else:
            total = part
    for d in range(1, ny):
        pltpu.make_async_remote_copy(
            src_ref=y_s.at[d - 1], dst_ref=y_r.at[d - 1], send_sem=y_ss.at[d - 1], recv_sem=y_rs.at[d - 1],
            device_id=(page, mate), device_id_type=MESH).wait_recv()
        total = total + y_r[d - 1].astype(F32)
    psend[...] = total.reshape(n_page, BEAMS, width).astype(BF16)
    precv[page] = psend[page]
    p_start, p_wait, p_done = page_copy(lambda p: psend.at[p], lambda p: precv.at[p], p_ss, p_rs)
    p_start()
    p_wait()
    ff = jnp.sum(precv[...].astype(F32), axis=0)
    for g in range(n_feat):
        fsend[g] = ff[g * home:(g + 1) * home]
    frecv[feat] = fsend[feat]
    f_start, f_wait, f_done = feat_copy(
        lambda p: fsend.at[p], lambda p: frecv.at[p], lambda p: f_ss.at[p], lambda p: f_rs.at[p])
    f_start()
    f_wait()
    square = jnp.zeros((home, 1), F32)
    for c in range(n_feat):
        v = frecv[c]
        square += jnp.sum(v * v, axis=1, keepdims=True)
    scale = lax.rsqrt(square / depth + EPS)
    for c in range(n_feat):
        base = jnp.zeros((home, width), F32)
        r8 = res[c]
        for g in range(n_feat):
            base = jnp.where(feat == g, r8[g * home:(g + 1) * home], base)
        v = base + frecv[c] * scale * gains_ref[2, c]
        out_ref[:, c * width:c * width + cut(c)] = v[:, 0:cut(c)].astype(BF16)

    q_done()
    st_done()
    n_done()
    lax.fori_loop(0, n_feat, lambda c, z: (pj(c)[2](), z)[1], 0)
    ag_done()
    for copy in sends:
        copy.wait_send()
    p_done()
    f_done()


def per_device(
    n_page, n_feat,
    queries, fresh_keys, fresh_values, paged_keys, paged_values, block_tables, parents, prompt_lengths,
    stream, output_matrix, attention_gain, feedforward_gain, gate_matrix, linear_matrix, down_matrix, closing_gain,
):
    depth = stream.shape[1]
    home = stream.shape[0]
    tiles = -(-depth // 128)
    width = -(-tiles // n_feat) * 128
    padded = width * n_feat
    rows = n_page * queries.shape[0]
    slots, page_len, kvw = paged_keys.shape
    hw = queries.shape[1]
    units = gate_matrix.shape[0]
    ny = n_feat // 2
    sb = slots * BEAMS

    tables = jnp.concatenate([block_tables, jnp.repeat(prompt_lengths, BEAMS)[:, None]], axis=1)
    chosen = parents[:, None] == jnp.arange(rows, dtype=jnp.int32)[None, :]
    by_row = jnp.sum(jnp.where(chosen[:, :, None], tables[None, :, :], 0), axis=1)
    by_col = jnp.sum(jnp.where(chosen.T[:, None, :], tables[:, :, None], 0), axis=0)
    gains = jnp.stack([attention_gain, feedforward_gain, closing_gain]).astype(F32)
    gains = jnp.pad(gains, ((0, 0), (0, padded - depth))).reshape(3, n_feat, 1, width)

    dma = pltpu.SemaphoreType.DMA
    scratch = [
        pltpu.VMEM(paged_keys.shape, BF16), pltpu.VMEM(paged_values.shape, BF16),
        pltpu.VMEM((n_feat, width, hw), BF16),
        pltpu.VMEM((n_feat, units, width), BF16), pltpu.VMEM((n_feat, units, width), BF16),
        pltpu.VMEM((n_feat, units, width), BF16),
        pltpu.VMEM((n_page, BEAMS, hw), BF16),
        pltpu.VMEM((sb, hw), F32),
        pltpu.VMEM((sb, HEAD), F32),
        pltpu.VMEM((sb, hw), F32),
        pltpu.VMEM((sb, HEAD), F32),
        pltpu.VMEM((n_page, BEAMS, hw + 2 * HEAD), BF16),
        pltpu.VMEM((n_page, BEAMS, hw + 2 * HEAD), BF16),
        pltpu.VMEM((BEAMS, hw), BF16),
        pltpu.VMEM((n_feat, home, padded), F32),
        pltpu.VMEM((n_feat, n_feat, BEAMS, width), BF16),
        pltpu.VMEM((n_feat, BEAMS, width), F32),
        pltpu.VMEM((n_feat, n_page, BEAMS, width), BF16),
        pltpu.VMEM((rows, width), BF16),
        pltpu.VMEM((rows, units), F32), pltpu.VMEM((rows, units), F32),
        pltpu.VMEM((rows, units), BF16),
        pltpu.VMEM((ny, rows, width), BF16), pltpu.VMEM((ny, rows, width), BF16),
        pltpu.VMEM((ny - 1, rows, width), BF16), pltpu.VMEM((ny - 1, rows, width), BF16),
        pltpu.VMEM((n_page, BEAMS, width), BF16), pltpu.VMEM((n_page, BEAMS, width), BF16),
        pltpu.VMEM((n_feat, home, width), F32), pltpu.VMEM((n_feat, home, width), F32),
        dma((2,)), dma((4, n_feat)),
        dma((n_page,)), dma((n_page,)),
        dma((n_page,)), dma((n_page,)),
        dma((n_feat,)), dma((n_feat,)),
        dma((n_feat, n_feat)), dma((n_feat, n_feat)),
        dma((n_page,)), dma((n_page,)),
        dma((ny,)), dma((ny,)), dma((n_feat,)),
        dma((ny,)), dma((ny,)), dma((ny - 1,)), dma((ny - 1,)),
        dma((n_page,)), dma((n_page,)),
        dma((n_feat,)), dma((n_feat,)),
    ]
    vmem = pl.BlockSpec(memory_space=pltpu.VMEM)
    hbm = pl.BlockSpec(memory_space=pl.ANY)
    return pl.pallas_call(
        functools.partial(layer_kernel, n_page, n_feat, width, depth),
        out_shape=jax.ShapeDtypeStruct((home, depth), BF16),
        in_specs=[vmem] * 7 + [hbm] * 6,
        out_specs=vmem,
        scratch_shapes=scratch,
        compiler_params=pltpu.CompilerParams(
            collective_id=0, has_side_effects=True, vmem_limit_bytes=60 * 2**20),
    )(queries, fresh_keys, fresh_values, by_col, by_row, stream, gains,
      paged_keys, paged_values, output_matrix, gate_matrix, linear_matrix, down_matrix)


def solution(mesh):
    both = P(("page", "feat"), None)
    placed = (
        P("page", "feat"), P("page", "feat"), P("page", "feat"),
        P("page", None, "feat"), P("page", None, "feat"),
        P(), P(), P(), both, P(None, "feat"), P(), P(), both, both, both, P(),
    )
    return jax.shard_map(
        functools.partial(per_device, mesh.shape["page"], mesh.shape["feat"]),
        mesh=mesh, in_specs=placed, out_specs=both, check_vma=False)
```

time: 345 us -> 81.2 us (0.24)
  waiting for transfers between devices: 150 us -> 0 us
  blocking collectives: 108 us -> 0 us
  Pallas kernels: 0 us -> 72.6 us
  matrix products: 35.1 us -> 0 us
  local copies, waits for them, and re-layouts: 27.2 us -> 5.7 us
  between operations: 14.7 us -> 0.02 us
  other arithmetic: 8.98 us -> 2.51 us
    unnamed x6 -> x0, waiting for transfers between devices: 101 us -> none
    pallas_call x0 -> x1, Pallas kernels: none -> 72.6 us  [per_device(): pl.pallas_call(functools.partial(layer_kernel, n_page, n_feat, width, dep...]
    all_gather x3 -> x0, blocking collectives: 70.5 us -> none  [the longest x1 32.3 us: per_device(): all_queries = lax.all_gather(queries, 'page', axis=0, tiled=True)]
    reduce_scatter x2 -> x0, waiting for transfers between devices: 49.4 us -> none  [the longest x1 25.9 us: per_device(): lax.psum_scatter(term_rows, 'feat', scatter_dimension=1, tiled=True)]
    unnamed x1 -> x0, blocking collectives: 37.1 us -> none
    dot_general x8 -> x0, matrix products: 35.1 us -> none  [the longest x1 12.6 us: per_device(): jnp.dot(hidden, down_matrix, preferred_element_type=jnp.float32)]
    reshape x7 -> x0, local copies, waits for them, and re-layouts: 16.6 us -> none  [the longest x1 6.93 us: per_device(): paged_values.reshape(slot_count, page_len, kv_heads, HEAD_DIM_SIZE)]
    gather x8 -> x0, local copies, waits for them, and re-layouts: 5.84 us -> none  [the longest x3 1.72 us: per_device(): row_in_use = jnp.take_along_axis(in_use, beam_rows, axis=1)]
  transfers between devices with their start and end apart: 4 -> 0, of which waited for: 4 -> 0; matrix products, arithmetic and copies ran while one was open for 1% -> 0% of each run, Pallas kernels for 0% -> 0%
where the time goes in v1:
time: 81.2 us; the launch traced here: 80.8 us
  Pallas kernels  72.6 us (89%)
  local copies, waits for them, and re-layouts  5.7 us (7%)
  other arithmetic  2.51 us (3%)
    pallas_call x1, Pallas kernels, per_device(): pl.pallas_call(functools.partial(layer_kernel, n_page, n_feat, width, dep...  72.6 us
    another operation x3, local copies, waits for them, and re-layouts, per_device(): jnp.stack([attention_gain, feedforward_gain, closing_gain]).astype(F32)  2.15 us
    unnamed x2, local copies, waits for them, and re-layouts  2.03 us

profile of v1, /device:TPU:0, one launch (start us, length us, event | category | flops | bytes accessed | tf_op | source)
XLA Modules:
  0.0 80.8 jit_solution(11559516083255778090)
XLA Ops:
  0.0 0.7 broadcast_in_dim.50
  0.7 0.1 broadcast_in_dim_reshape.3
  0.8 0.7 constant_dynamic-update-slice_fusion
  1.5 0.8 iota_compare_fusion
  2.3 0.2 select_reduce_fusion
  2.6 0.8 select_reduce_fusion.1.by_col_ref
  3.3 0.7 stack.16
  4.1 0.7 stack.17
  4.8 0.7 stack.18
  5.5 0.7 maximum_convert_fusion.gains_ref
  6.2 0.7 copy.27.by_row_ref
  6.9 72.6 %shard_map.154 = bf16[2,4608]{1,0:T(2,128)(2,1)} custom-call(bf16[8,1024]{1,0:T(8,128)(2,1)} %q_ref.1, bf16[8,512]{1,0:T(8,128)(2,1)} %fk_ref.1, bf16[8,512]{1,0:T(8,128)(2,1)} %fv_ref.1, s32[9,64]{1,0:T(8,128)} %select_reduce_fusion.1.by_col_ref, s32[64,9]{1,0:T(8,128)} %copy.27.by_row_ref, bf16[2,4608]{1,0:T(2,128)(2,1)} %stream_ref.1, ...), custom_call_target="tpu_custom_call" | custom-call | tf_op jit(solution)/shard_map/pallas_call | solution.py:441
  79.5 1.3 %copy.30 = bf16[2,4608]{1,0:T(2,128)(2,1)} copy(bf16[2,4608]{1,0:T(2,128)(2,1)} %shard_map.154) | data formatting | bytes 36864
  (1 shorter events, 0.0 us)

commit v2 on v1

--- a/solution.py
+++ b/solution.py
@@ -19,6 +19,7 @@
 MESH = pl.DeviceIdType.MESH
 NT = (((1,), (1,)), ((), ()))
 NN = (((1,), (0,)), ((), ()))
+TN = (((0,), (0,)), ((), ()))
 
 
 def capped_exp(raw):
@@ -31,11 +32,11 @@
 
 def layer_kernel(
     n_page, n_feat, width, depth,
-    q_ref, fk_ref, fv_ref, by_col_ref, by_row_ref, stream_ref, gains_ref,
+    q_ref, fk_ref, fv_ref, tables_ref, parents_ref, lengths_ref, stream_ref, gains_ref,
     keys_hbm, values_hbm, wo_hbm, gate_hbm, lift_hbm, down_hbm,
     out_ref,
     kbuf, vbuf, wo, gate, lift, down,
-    allq, qs, nvs, snum, stot, nsend, nrecv, att, strm, prj, res,
+    by_row, row_lens, allq, qs, nvs, snum, stot, nsend, nrecv, att, strm, prj, res,
     xg, xs, gacc, uacc, hid, core_s, core_r, y_s, y_r, psend, precv, fsend, frecv,
     kv_sem, w_sem,
     q_ss, q_rs, n_ss, n_rs, st_ss, st_rs, pj_ss, pj_rs, ag_ss, ag_rs,
@@ -77,9 +78,6 @@
             down[c, :, cut(c):] = jnp.zeros((gate.shape[1], rest), BF16)
     for copy in local:
         copy.start()
-    for kind in w_copies:
-        for copy in kind:
-            copy.start()
 
     barrier = pltpu.get_barrier_semaphore()
 
@@ -155,33 +153,33 @@
         lambda p: strm.at[feat], lambda p: strm.at[p], lambda p: st_ss.at[p], lambda p: st_rs.at[p])
     st_start()
 
-    blocks = by_col_ref.shape[0] - 1
+    def one_row(r, z):
+        by_row[pl.ds(r, 1), :] = tables_ref[pl.ds(parents_ref[r], 1), :]
+        row_lens[pl.ds(r, 1), :] = jnp.full((1, HEAD), lengths_ref[r // BEAMS], jnp.int32)
+        return z
+
+    lax.fori_loop(0, rows, one_row, 0, unroll=8)
+    blocks = tables_ref.shape[1]
     sb = slots * BEAMS
-    down_i = lax.broadcasted_iota(jnp.int32, (sb, rows), 0)
-    across = lax.broadcasted_iota(jnp.int32, (sb, rows), 1)
-    seen = jnp.zeros((sb, rows), jnp.int32)
-    lens = by_col_ref[blocks:blocks + 1, :]
+    row_i = lax.broadcasted_iota(jnp.int32, (rows, sb), 0)
+    spot_i = lax.broadcasted_iota(jnp.int32, (rows, sb), 1)
+    lens = row_lens[:, 0:1]
+    seen = jnp.zeros((rows, sb), jnp.int32)
     for b in range(blocks):
-        seen += jnp.where(by_col_ref[b:b + 1, :] == page * slots + down_i // BEAMS,
+        seen += jnp.where(by_row[:, b:b + 1] == page * slots + spot_i // BEAMS,
                           jnp.clip(lens - b * page_len, 0, page_len), 0)
-    seen = jnp.where(across % BEAMS == down_i % BEAMS, seen, 0).astype(F32)
-    pick = jnp.where(seen > 0, 1.0, 0.0).astype(BF16)
-    nvs[...] = jnp.broadcast_to(jnp.sum(seen, axis=1, keepdims=True), nvs.shape)
-
-    down_t = lax.broadcasted_iota(jnp.int32, (rows, sb), 0)
-    across_t = lax.broadcasted_iota(jnp.int32, (rows, sb), 1)
-    seen_t = jnp.zeros((rows, sb), jnp.int32)
-    lens_t = by_row_ref[:, blocks:blocks + 1]
-    for b in range(blocks):
-        seen_t += jnp.where(by_row_ref[:, b:b + 1] == page * slots + across_t // BEAMS,
-                            jnp.clip(lens_t - b * page_len, 0, page_len), 0)
-    pick_t = jnp.where(jnp.logical_and(across_t % BEAMS == down_t % BEAMS, seen_t > 0), 1.0, 0.0).astype(BF16)
+    seen = jnp.where(spot_i % BEAMS == row_i % BEAMS, seen, 0).astype(F32)
+    pick_t = jnp.where(seen > 0, 1.0, 0.0).astype(BF16)
+    nvs[...] = mm(seen.astype(BF16), jnp.ones((rows, HEAD), BF16), TN)
 
     q_wait()
     q_all = allq[...].astype(F32).reshape(rows, hw).astype(BF16)
-    qs[...] = mm(pick, q_all, NN)
+    qs[...] = mm(pick_t, q_all, TN)
     for copy in local:
         copy.wait()
+    for kind in w_copies:
+        for copy in kind:
+            copy.start()
 
     lane = lax.broadcasted_iota(jnp.int32, (BEAMS, HEAD), 1)
     position = lax.broadcasted_iota(jnp.int32, (groups * BEAMS, page_len), 1).astype(F32)
@@ -393,10 +391,6 @@
     ny = n_feat // 2
     sb = slots * BEAMS
 
-    tables = jnp.concatenate([block_tables, jnp.repeat(prompt_lengths, BEAMS)[:, None]], axis=1)
-    chosen = parents[:, None] == jnp.arange(rows, dtype=jnp.int32)[None, :]
-    by_row = jnp.sum(jnp.where(chosen[:, :, None], tables[None, :, :], 0), axis=1)
-    by_col = jnp.sum(jnp.where(chosen.T[:, None, :], tables[:, :, None], 0), axis=0)
     gains = jnp.stack([attention_gain, feedforward_gain, closing_gain]).astype(F32)
     gains = jnp.pad(gains, ((0, 0), (0, padded - depth))).reshape(3, n_feat, 1, width)
 
@@ -406,6 +400,7 @@
         pltpu.VMEM((n_feat, width, hw), BF16),
         pltpu.VMEM((n_feat, units, width), BF16), pltpu.VMEM((n_feat, units, width), BF16),
         pltpu.VMEM((n_feat, units, width), BF16),
+        pltpu.VMEM((rows, block_tables.shape[1]), jnp.int32), pltpu.VMEM((rows, HEAD), jnp.int32),
         pltpu.VMEM((n_page, BEAMS, hw), BF16),
         pltpu.VMEM((sb, hw), F32),
         pltpu.VMEM((sb, HEAD), F32),
@@ -437,16 +432,17 @@
         dma((n_feat,)), dma((n_feat,)),
     ]
     vmem = pl.BlockSpec(memory_space=pltpu.VMEM)
+    smem = pl.BlockSpec(memory_space=pltpu.SMEM)
     hbm = pl.BlockSpec(memory_space=pl.ANY)
     return pl.pallas_call(
         functools.partial(layer_kernel, n_page, n_feat, width, depth),
         out_shape=jax.ShapeDtypeStruct((home, depth), BF16),
-        in_specs=[vmem] * 7 + [hbm] * 6,
+        in_specs=[vmem] * 4 + [smem] * 2 + [vmem] * 2 + [hbm] * 6,
         out_specs=vmem,
         scratch_shapes=scratch,
         compiler_params=pltpu.CompilerParams(
             collective_id=0, has_side_effects=True, vmem_limit_bytes=60 * 2**20),
-    )(queries, fresh_keys, fresh_values, by_col, by_row, stream, gains,
+    )(queries, fresh_keys, fresh_values, block_tables, parents, prompt_lengths, stream, gains,
       paged_keys, paged_values, output_matrix, gate_matrix, linear_matrix, down_matrix)
 
 

time: 81.2 us -> 70.7 us (0.87)
  Pallas kernels: 72.6 us -> 64.7 us
  other arithmetic: 2.51 us -> 0.7 us
  local copies, waits for them, and re-layouts: 5.7 us -> 4.86 us
    pallas_call x1, Pallas kernels: 72.6 us -> 64.7 us  [per_device(): pl.pallas_call(functools.partial(layer_kernel, n_page, n_feat, width, dep...]
    reduce_sum x2 -> x0, other arithmetic: 1 us -> none  [the longest x1 0.76 us: per_device(): jnp.sum(jnp.where(chosen.T[:, None, :], tables[:, :, None], 0), axis=0)]
where the time goes in v2:
time: 70.7 us; the launch traced here: 70.3 us
  Pallas kernels  64.7 us (92%)
  local copies, waits for them, and re-layouts  4.86 us (7%)
    pallas_call x1, Pallas kernels, per_device(): pl.pallas_call(functools.partial(layer_kernel, n_page, n_feat, width, dep...  64.7 us
    unnamed x2, local copies, waits for them, and re-layouts  2.71 us
    another operation x3, local copies, waits for them, and re-layouts, per_device(): jnp.stack([attention_gain, feedforward_gain, closing_gain]).astype(F32)  2.15 us

profile of v2, /device:TPU:0, one launch (start us, length us, event | category | flops | bytes accessed | tf_op | source)
XLA Modules:
  0.0 70.3 jit_solution(2637075717605174544)
XLA Ops:
  0.0 0.7 %stack.16 = bf16[1,4,1,1152]{3,2,1,0:T(2,128)(2,1)S(1)} reshape(bf16[4608]{0:T(1024)(128)(2,1)} %param.26) | data formatting | bytes 18432 | tf_op jit(solution)/shard_map/stack | solution.py:394
  0.7 0.7 %stack.17 = bf16[1,4,1,1152]{3,2,1,0:T(2,128)(2,1)S(1)} reshape(bf16[4608]{0:T(1024)(128)(2,1)} %param.27) | data formatting | bytes 18432 | tf_op jit(solution)/shard_map/stack | solution.py:394
  1.4 0.7 %stack.18 = bf16[1,4,1,1152]{3,2,1,0:T(2,128)(2,1)S(1)} reshape(bf16[4608]{0:T(1024)(128)(2,1)} %param.31) | data formatting | bytes 18432 | tf_op jit(solution)/shard_map/stack | solution.py:394
  2.2 0.7 maximum_convert_fusion.gains_ref
  2.9 1.4 %copy.21.tables_ref = s32[64,8]{1,0:T(8,128)} copy(s32[64,8]{0,1:T(8,128)} %param.21) | data formatting | bytes 4096 | tf_op args[5]
  4.2 64.7 %shard_map.154 = bf16[2,4608]{1,0:T(2,128)(2,1)} custom-call(bf16[8,1024]{1,0:T(8,128)(2,1)} %q_ref.1, bf16[8,512]{1,0:T(8,128)(2,1)} %fk_ref.1, bf16[8,512]{1,0:T(8,128)(2,1)} %fv_ref.1, s32[64,8]{1,0:T(8,128)} %copy.21.tables_ref, s32[64]{0:T(128)} %parents_ref.1, s32[8]{0:T(128)} %lengths_ref.1, bf16[2,4608]{1,0:T(2,128)(2,1)} %stream_ref.1, ...), custom_call_target="tpu_custom_call" | custom-call | tf_op jit(solution)/shard_map/pallas_call | solution.py:437
  68.9 1.3 %copy.23 = bf16[2,4608]{1,0:T(2,128)(2,1)} copy(bf16[2,4608]{1,0:T(2,128)(2,1)} %shard_map.154) | data formatting | bytes 36864

commit v3 on v2

--- a/solution.py
+++ b/solution.py
@@ -36,7 +36,7 @@
     keys_hbm, values_hbm, wo_hbm, gate_hbm, lift_hbm, down_hbm,
     out_ref,
     kbuf, vbuf, wo, gate, lift, down,
-    by_row, row_lens, allq, qs, nvs, snum, stot, nsend, nrecv, att, strm, prj, res,
+    allq, qs, nvs, snum, stot, nsend, nrecv, att, strm, prj, res,
     xg, xs, gacc, uacc, hid, core_s, core_r, y_s, y_r, psend, precv, fsend, frecv,
     kv_sem, w_sem,
     q_ss, q_rs, n_ss, n_rs, st_ss, st_rs, pj_ss, pj_rs, ag_ss, ag_rs,
@@ -54,6 +54,10 @@
     rows = n_page * BEAMS
     home = stream_ref.shape[0]
     hw = heads * HEAD
+
+    def gain(i, c):
+        first = (i * n_feat + c) * width
+        return gains_ref[:, first:first + width]
 
     def cut(c):
         return min(width, depth - c * width)
@@ -153,28 +157,30 @@
         lambda p: strm.at[feat], lambda p: strm.at[p], lambda p: st_ss.at[p], lambda p: st_rs.at[p])
     st_start()
 
-    def one_row(r, z):
-        by_row[pl.ds(r, 1), :] = tables_ref[pl.ds(parents_ref[r], 1), :]
-        row_lens[pl.ds(r, 1), :] = jnp.full((1, HEAD), lengths_ref[r // BEAMS], jnp.int32)
-        return z
-
-    lax.fori_loop(0, rows, one_row, 0, unroll=8)
-    blocks = tables_ref.shape[1]
+    blocks = tables_ref.shape[0]
+    prompts = lengths_ref.shape[1]
     sb = slots * BEAMS
-    row_i = lax.broadcasted_iota(jnp.int32, (rows, sb), 0)
-    spot_i = lax.broadcasted_iota(jnp.int32, (rows, sb), 1)
-    lens = row_lens[:, 0:1]
-    seen = jnp.zeros((rows, sb), jnp.int32)
+    chosen = lax.broadcasted_iota(jnp.int32, (rows, rows), 0) == parents_ref[...]
+    by_col = lax.dot_general(tables_ref[...].astype(F32), jnp.where(chosen, 1.0, 0.0), NN,
+                             precision=lax.Precision.HIGHEST, preferred_element_type=F32)
+    of_prompt = (lax.broadcasted_iota(jnp.int32, (prompts, rows), 0)
+                 == lax.broadcasted_iota(jnp.int32, (prompts, rows), 1) // BEAMS)
+    lens = lax.dot_general(lengths_ref[...].astype(F32), jnp.where(of_prompt, 1.0, 0.0), NN,
+                           precision=lax.Precision.HIGHEST, preferred_element_type=F32)
+    spot_i = lax.broadcasted_iota(jnp.int32, (sb, rows), 0)
+    row_i = lax.broadcasted_iota(jnp.int32, (sb, rows), 1)
+    slot_id = (page * slots + spot_i // BEAMS).astype(F32)
+    seen = jnp.zeros((sb, rows), F32)
     for b in range(blocks):
-        seen += jnp.where(by_row[:, b:b + 1] == page * slots + spot_i // BEAMS,
-                          jnp.clip(lens - b * page_len, 0, page_len), 0)
-    seen = jnp.where(spot_i % BEAMS == row_i % BEAMS, seen, 0).astype(F32)
-    pick_t = jnp.where(seen > 0, 1.0, 0.0).astype(BF16)
-    nvs[...] = mm(seen.astype(BF16), jnp.ones((rows, HEAD), BF16), TN)
+        seen += jnp.where(jnp.abs(by_col[b:b + 1, :] - slot_id) < 0.5,
+                          jnp.clip(lens - b * page_len, 0.0, float(page_len)), 0.0)
+    seen = jnp.where(spot_i % BEAMS == row_i % BEAMS, seen, 0.0)
+    pick = jnp.where(seen > 0, 1.0, 0.0).astype(BF16)
+    nvs[...] = jnp.broadcast_to(jnp.sum(seen, axis=1, keepdims=True), nvs.shape)
 
     q_wait()
     q_all = allq[...].astype(F32).reshape(rows, hw).astype(BF16)
-    qs[...] = mm(pick_t, q_all, TN)
+    qs[...] = mm(pick, q_all, NN)
     for copy in local:
         copy.wait()
     for kind in w_copies:
@@ -215,7 +221,7 @@
     def to_rows(v):
         hi = v.astype(BF16)
         lo = (v - hi.astype(F32)).astype(BF16)
-        return mm(pick_t, hi, NN) + mm(pick_t, lo, NN)
+        return mm(pick, hi, TN) + mm(pick, lo, TN)
 
     tot_rows = to_rows(stot[...])
     tot_hi = tot_rows.astype(BF16)
@@ -267,11 +273,14 @@
     for c in range(n_feat):
         cols = slice(c * width, (c + 1) * width)
         base = jnp.concatenate([strm[g, :, cols] for g in range(n_feat)], axis=0)
-        v = base + res[c] * scale * gains_ref[0, c]
+        v = base + res[c] * scale * gain(0, c)
         res[c] = v
         square += jnp.sum(v * v, axis=1, keepdims=True)
     scale = lax.rsqrt(square / depth + EPS)
-    xg[feat, page] = (res[feat] * scale * gains_ref[1, feat]).astype(BF16)
+    own_gain = gain(1, 0)
+    for c in range(1, n_feat):
+        own_gain = jnp.where(feat == c, gain(1, c), own_gain)
+    xg[feat, page] = (res[feat] * scale * own_gain).astype(BF16)
 
     ag_start, ag_wait, ag_done = page_copy(
         lambda p: xg.at[feat, page], lambda p: xg.at[feat, p], ag_ss, ag_rs)
@@ -302,12 +311,15 @@
                 sends[-1].start()
             xs[...] = xg[q].astype(F32).reshape(rows, width).astype(BF16)
             if d or o:
-                gacc[...] += mm(xs[...], gate[q], NT)
-                uacc[...] += mm(xs[...], lift[q], NT)
+                gacc[...] += mm(gate[q], xs[...], NT)
+                uacc[...] += mm(lift[q], xs[...], NT)
             else:
-                gacc[...] = mm(xs[...], gate[q], NT)
-                uacc[...] = mm(xs[...], lift[q], NT)
-    hid[...] = (jax.nn.gelu(gacc[...], approximate=True) * uacc[...]).astype(BF16)
+                gacc[...] = mm(gate[q], xs[...], NT)
+                uacc[...] = mm(lift[q], xs[...], NT)
+    turned = (jax.nn.gelu(gacc[...], approximate=True) * uacc[...]).astype(BF16)
+    eye = jnp.where(lax.broadcasted_iota(jnp.int32, (rows, rows), 0)
+                    == lax.broadcasted_iota(jnp.int32, (rows, rows), 1), 1.0, 0.0).astype(BF16)
+    hid[...] = mm(eye, turned, NT).astype(BF16)
 
     for copy in w_copies[3]:
         copy.wait()
@@ -360,7 +372,7 @@
         r8 = res[c]
         for g in range(n_feat):
             base = jnp.where(feat == g, r8[g * home:(g + 1) * home], base)
-        v = base + frecv[c] * scale * gains_ref[2, c]
+        v = base + frecv[c] * scale * gain(2, c)
         out_ref[:, c * width:c * width + cut(c)] = v[:, 0:cut(c)].astype(BF16)
 
     q_done()
@@ -391,8 +403,9 @@
     ny = n_feat // 2
     sb = slots * BEAMS
 
-    gains = jnp.stack([attention_gain, feedforward_gain, closing_gain]).astype(F32)
-    gains = jnp.pad(gains, ((0, 0), (0, padded - depth))).reshape(3, n_feat, 1, width)
+    gains = jnp.concatenate([
+        jnp.pad(g.astype(F32), (0, padded - depth)) if padded > depth else g.astype(F32)
+        for g in (attention_gain, feedforward_gain, closing_gain)]).reshape(1, -1)
 
     dma = pltpu.SemaphoreType.DMA
     scratch = [
@@ -400,7 +413,6 @@
         pltpu.VMEM((n_feat, width, hw), BF16),
         pltpu.VMEM((n_feat, units, width), BF16), pltpu.VMEM((n_feat, units, width), BF16),
         pltpu.VMEM((n_feat, units, width), BF16),
-        pltpu.VMEM((rows, block_tables.shape[1]), jnp.int32), pltpu.VMEM((rows, HEAD), jnp.int32),
         pltpu.VMEM((n_page, BEAMS, hw), BF16),
         pltpu.VMEM((sb, hw), F32),
         pltpu.VMEM((sb, HEAD), F32),
@@ -414,7 +426,7 @@
         pltpu.VMEM((n_feat, BEAMS, width), F32),
         pltpu.VMEM((n_feat, n_page, BEAMS, width), BF16),
         pltpu.VMEM((rows, width), BF16),
-        pltpu.VMEM((rows, units), F32), pltpu.VMEM((rows, units), F32),
+        pltpu.VMEM((units, rows), F32), pltpu.VMEM((units, rows), F32),
         pltpu.VMEM((rows, units), BF16),
         pltpu.VMEM((ny, rows, width), BF16), pltpu.VMEM((ny, rows, width), BF16),
         pltpu.VMEM((ny - 1, rows, width), BF16), pltpu.VMEM((ny - 1, rows, width), BF16),
@@ -432,17 +444,17 @@
         dma((n_feat,)), dma((n_feat,)),
     ]
     vmem = pl.BlockSpec(memory_space=pltpu.VMEM)
-    smem = pl.BlockSpec(memory_space=pltpu.SMEM)
     hbm = pl.BlockSpec(memory_space=pl.ANY)
     return pl.pallas_call(
         functools.partial(layer_kernel, n_page, n_feat, width, depth),
         out_shape=jax.ShapeDtypeStruct((home, depth), BF16),
-        in_specs=[vmem] * 4 + [smem] * 2 + [vmem] * 2 + [hbm] * 6,
+        in_specs=[vmem] * 8 + [hbm] * 6,
         out_specs=vmem,
         scratch_shapes=scratch,
         compiler_params=pltpu.CompilerParams(
             collective_id=0, has_side_effects=True, vmem_limit_bytes=60 * 2**20),
-    )(queries, fresh_keys, fresh_values, block_tables, parents, prompt_lengths, stream, gains,
+    )(queries, fresh_keys, fresh_values, block_tables.T, parents.reshape(1, -1),
+      prompt_lengths.reshape(1, -1), stream, gains,
       paged_keys, paged_values, output_matrix, gate_matrix, linear_matrix, down_matrix)
 
 

time: 70.7 us -> 67.8 us (0.959)
  local copies, waits for them, and re-layouts: 4.86 us -> 2 us
    another operation x3 -> x0, local copies, waits for them, and re-layouts: 2.15 us -> none  [per_device(): jnp.stack([attention_gain, feedforward_gain, closing_gain]).astype(F32)]
    unnamed x2 -> x1, local copies, waits for them, and re-layouts: 2.71 us -> 1.34 us
    reshape x0 -> x1, other arithmetic: none -> 0.74 us  [per_device(): gains = jnp.concatenate([jnp.pad(g.astype(F32), (0, padded - depth)) if p...]
where the time goes in v3:
time: 67.8 us; the launch traced here: 67.5 us
  Pallas kernels  64.8 us (96%)
  local copies, waits for them, and re-layouts  2 us (3%)
  other arithmetic  0.74 us (1%)
    pallas_call x1, Pallas kernels, per_device(): pl.pallas_call(functools.partial(layer_kernel, n_page, n_feat, width, dep...  64.8 us

profile of v3, /device:TPU:0, one launch (start us, length us, event | category | flops | bytes accessed | tf_op | source)
XLA Modules:
  0.0 67.5 jit_solution(14124754354461253970)
XLA Ops:
  0.0 0.7 %maximum_convert_fusion = f32[13824]{0:T(1024)S(1)} fusion(bf16[4608]{0:T(1024)(128)(2,1)} %param.31, bf16[4608]{0:T(1024)(128)(2,1)} %param.27, bf16[4608]{0:T(1024)(128)(2,1)} %param.26), kind=kLoop, calls=%fused_computation | loop fusion | flops 82944 | bytes 82944 | tf_op jit(solution)/shard_map/reshape | solution.py:408
  0.7 0.7 reshape.16.gains_ref
  1.4 64.8 %shard_map.154 = bf16[2,4608]{1,0:T(2,128)(2,1)} custom-call(bf16[8,1024]{1,0:T(8,128)(2,1)} %q_ref.1, bf16[8,512]{1,0:T(8,128)(2,1)} %fk_ref.1, bf16[8,512]{1,0:T(8,128)(2,1)} %fv_ref.1, s32[8,64]{1,0:T(8,128)} %bitcast.3, s32[1,64]{1,0:T(1,128)} %bitcast.4, s32[1,8]{1,0:T(1,128)} %bitcast.5, bf16[2,4608]{1,0:T(2,128)(2,1)} %stream_ref.1, ...), custom_call_target="tpu_custom_call" | custom-call | tf_op jit(solution)/shard_map/pallas_call | solution.py:448
  66.2 1.3 %copy.18 = bf16[2,4608]{1,0:T(2,128)(2,1)} copy(bf16[2,4608]{1,0:T(2,128)(2,1)} %shard_map.154) | data formatting | bytes 36864

commit v4 on v3

--- a/solution.py
+++ b/solution.py
@@ -24,6 +24,15 @@
 
 def capped_exp(raw):
     return jnp.exp(SOFTCAP * jnp.tanh(raw * (1.0 / (math.sqrt(QSCALAR) * SOFTCAP))))
+
+
+def ahead(i, d, n):
+    return jnp.where(i + d >= n, i + d - n, i + d)
+
+
+def halves(width):
+    first = width // 512 * 256
+    return ((0, first), (first, width - first)) if first else ((0, width),)
 
 
 def mm(a, b, dims):
@@ -37,7 +46,7 @@
     out_ref,
     kbuf, vbuf, wo, gate, lift, down,
     allq, qs, nvs, snum, stot, nsend, nrecv, att, strm, prj, res,
-    xg, xs, gacc, uacc, hid, core_s, core_r, y_s, y_r, psend, precv, fsend, frecv,
+    xg, gacc, uacc, hid, core_s, core_r, y_s, y_r, psend, precv, fsend, frecv,
     kv_sem, w_sem,
     q_ss, q_rs, n_ss, n_rs, st_ss, st_rs, pj_ss, pj_rs, ag_ss, ag_rs,
     xy_ss, xc_ss, x_rs, c_ss, c_rs, y_ss, y_rs, p_ss, p_rs, f_ss, f_rs,
@@ -54,6 +63,9 @@
     rows = n_page * BEAMS
     home = stream_ref.shape[0]
     hw = heads * HEAD
+
+    spans = [pl.ds(first, size) for first, size in halves(width)]
+    parts = len(spans)
 
     def gain(i, c):
         first = (i * n_feat + c) * width
@@ -86,11 +98,11 @@
     barrier = pltpu.get_barrier_semaphore()
 
     def greet_page(d, _):
-        pl.semaphore_signal(barrier, inc=1, device_id=((page + d) % n_page, feat), device_id_type=MESH)
+        pl.semaphore_signal(barrier, inc=1, device_id=(ahead(page, d, n_page), feat), device_id_type=MESH)
         return 0
 
     def greet_feat(d, _):
-        pl.semaphore_signal(barrier, inc=1, device_id=(page, (feat + d) % n_feat), device_id_type=MESH)
+        pl.semaphore_signal(barrier, inc=1, device_id=(page, ahead(feat, d, n_feat)), device_id_type=MESH)
         return 0
 
     lax.fori_loop(1, n_page, greet_page, 0)
@@ -105,49 +117,49 @@
 
     def page_copy(src, dst, ss, rs):
         def send(d):
-            peer = (page + d) % n_page
+            peer = ahead(page, d, n_page)
             return pltpu.make_async_remote_copy(
                 src_ref=src(peer), dst_ref=dst(page), send_sem=ss.at[peer], recv_sem=rs.at[page],
                 device_id=(peer, feat), device_id_type=MESH)
 
         def arrival(d):
-            peer = (page + d) % n_page
+            peer = ahead(page, d, n_page)
             return pltpu.make_async_remote_copy(
                 src_ref=src(peer), dst_ref=dst(peer), send_sem=ss.at[peer], recv_sem=rs.at[peer],
                 device_id=(peer, feat), device_id_type=MESH)
 
         def start():
-            lax.fori_loop(1, n_page, lambda d, z: (send(d).start(), z)[1], 0)
+            lax.fori_loop(1, n_page, lambda d, z: (send(d).start(), z)[1], 0, unroll=n_page <= 8)
 
         def wait_recv():
-            lax.fori_loop(1, n_page, lambda d, z: (arrival(d).wait_recv(), z)[1], 0)
+            lax.fori_loop(1, n_page, lambda d, z: (arrival(d).wait_recv(), z)[1], 0, unroll=n_page <= 8)
 
         def wait_send():
-            lax.fori_loop(1, n_page, lambda d, z: (send(d).wait_send(), z)[1], 0)
+            lax.fori_loop(1, n_page, lambda d, z: (send(d).wait_send(), z)[1], 0, unroll=n_page <= 8)
 
         return start, wait_recv, wait_send
 
     def feat_copy(src, dst, ss, rs):
         def send(d):
-            peer = (feat + d) % n_feat
+            peer = ahead(feat, d, n_feat)
             return pltpu.make_async_remote_copy(
                 src_ref=src(peer), dst_ref=dst(feat), send_sem=ss(peer), recv_sem=rs(feat),
                 device_id=(page, peer), device_id_type=MESH)
 
         def arrival(d):
-            peer = (feat + d) % n_feat
+            peer = ahead(feat, d, n_feat)
             return pltpu.make_async_remote_copy(
                 src_ref=src(peer), dst_ref=dst(peer), send_sem=ss(peer), recv_sem=rs(peer),
                 device_id=(page, peer), device_id_type=MESH)
 
         def start():
-            lax.fori_loop(1, n_feat, lambda d, z: (send(d).start(), z)[1], 0)
+            lax.fori_loop(1, n_feat, lambda d, z: (send(d).start(), z)[1], 0, unroll=n_feat <= 8)
 
         def wait_recv():
-            lax.fori_loop(1, n_feat, lambda d, z: (arrival(d).wait_recv(), z)[1], 0)
+            lax.fori_loop(1, n_feat, lambda d, z: (arrival(d).wait_recv(), z)[1], 0, unroll=n_feat <= 8)
 
         def wait_send():
-            lax.fori_loop(1, n_feat, lambda d, z: (send(d).wait_send(), z)[1], 0)
+            lax.fori_loop(1, n_feat, lambda d, z: (send(d).wait_send(), z)[1], 0, unroll=n_feat <= 8)
 
         return start, wait_recv, wait_send
 
@@ -187,6 +199,7 @@
         for copy in kind:
             copy.start()
 
+    half_lanes = HEAD // 2
     lane = lax.broadcasted_iota(jnp.int32, (BEAMS, HEAD), 1)
     position = lax.broadcasted_iota(jnp.int32, (groups * BEAMS, page_len), 1).astype(F32)
 
@@ -206,10 +219,10 @@
             for g in range(groups):
                 h = k * groups + g
                 snum[at, h * HEAD:(h + 1) * HEAD] = num[g * BEAMS:(g + 1) * BEAMS]
-                sums = jnp.where(lane == h, tot[g * BEAMS:(g + 1) * BEAMS], sums)
+                sums = jnp.where(lane % half_lanes == h, tot[g * BEAMS:(g + 1) * BEAMS], sums)
         stot[at, :] = sums
 
-    per = 2 if slots % 2 == 0 else 1
+    per = 4 if slots % 4 == 0 else 1
 
     def some_slots(i, z):
         for u in range(per):
@@ -224,11 +237,11 @@
         return mm(pick, hi, TN) + mm(pick, lo, TN)
 
     tot_rows = to_rows(stot[...])
-    tot_hi = tot_rows.astype(BF16)
-    tot_lo = tot_rows - tot_hi.astype(F32)
+    tot_hi = tot_rows.astype(BF16).astype(F32)
+    first = lax.broadcasted_iota(jnp.int32, tot_rows.shape, 1) < half_lanes
+    tot_both = jnp.where(first, tot_hi, tot_rows - tot_hi)
     nsend[:, :, 0:hw] = to_rows(snum[...]).reshape(n_page, BEAMS, hw).astype(BF16)
-    nsend[:, :, hw:hw + HEAD] = tot_hi.astype(F32).reshape(n_page, BEAMS, HEAD).astype(BF16)
-    nsend[:, :, hw + HEAD:hw + 2 * HEAD] = tot_lo.reshape(n_page, BEAMS, HEAD).astype(BF16)
+    nsend[:, :, hw:hw + HEAD] = tot_both.reshape(n_page, BEAMS, HEAD).astype(BF16)
     nrecv[page] = nsend[page]
     n_start, n_wait, n_done = page_copy(lambda p: nsend.at[p], lambda p: nrecv.at[p], n_ss, n_rs)
     n_start()
@@ -239,13 +252,13 @@
         qk = q_ref[:, h * HEAD:(h + 1) * HEAD].astype(F32) * fk_ref[:, k * HEAD:(k + 1) * HEAD].astype(F32)
         own_w.append(capped_exp(jnp.sum(qk, axis=1, keepdims=True)))
     n_wait()
-    totals = jnp.sum(nrecv[:, :, hw:hw + HEAD].astype(F32) + nrecv[:, :, hw + HEAD:hw + 2 * HEAD].astype(F32), axis=0)
+    totals = jnp.sum(nrecv[:, :, hw:hw + HEAD].astype(F32), axis=0)
     for h in range(heads):
         k = h // groups
         hs = slice(h * HEAD, (h + 1) * HEAD)
         num = jnp.sum(nrecv[:, :, hs].astype(F32), axis=0)
         num += own_w[h].astype(BF16).astype(F32) * fv_ref[:, k * HEAD:(k + 1) * HEAD].astype(F32)
-        att[:, hs] = (num / (totals[:, h:h + 1] + own_w[h])).astype(BF16)
+        att[:, hs] = (num / (totals[:, h:h + 1] + totals[:, half_lanes + h:half_lanes + h + 1] + own_w[h])).astype(BF16)
 
     for copy in w_copies[0]:
         copy.wait()
@@ -282,78 +295,97 @@
         own_gain = jnp.where(feat == c, gain(1, c), own_gain)
     xg[feat, page] = (res[feat] * scale * own_gain).astype(BF16)
 
-    ag_start, ag_wait, ag_done = page_copy(
-        lambda p: xg.at[feat, page], lambda p: xg.at[feat, p], ag_ss, ag_rs)
-    ag_start()
+    def ag(i):
+        return page_copy(lambda p: xg.at[feat, page, :, spans[i]], lambda p: xg.at[feat, p, :, spans[i]],
+                         ag_ss.at[i], ag_rs.at[i])
+
+    for i in range(parts):
+        ag(i)[0]()
     for kind in w_copies[1:3]:
         for copy in kind:
             copy.wait()
 
-    def chunk_copy(q, peer, ss):
+    def chunk_copy(q, i, peer, ss):
         return pltpu.make_async_remote_copy(
-            src_ref=xg.at[q], dst_ref=xg.at[q], send_sem=ss, recv_sem=x_rs.at[q],
+            src_ref=xg.at[q, :, :, spans[i]], dst_ref=xg.at[q, :, :, spans[i]], send_sem=ss, recv_sem=x_rs.at[q, i],
             device_id=(page, peer), device_id_type=MESH)
 
-    ag_wait()
     sends = []
+
+    def absorb(q, i, fresh):
+        sp = spans[i]
+        x = xg[q, :, :, sp].astype(F32).reshape(rows, sp.size).astype(BF16)
+        if fresh:
+            gacc[...] = mm(x, gate[q, :, sp], NT)
+            uacc[...] = mm(x, lift[q, :, sp], NT)
+        else:
+            gacc[...] += mm(x, gate[q, :, sp], NT)
+            uacc[...] += mm(x, lift[q, :, sp], NT)
+
+    for i in range(parts):
+        ag(i)[1]()
+        for d in range(1, ny):
+            sends.append(chunk_copy(feat, i, ahead(yy, d, ny) * 2 + cc, xy_ss.at[d, i]))
+            sends[-1].start()
+        sends.append(chunk_copy(feat, i, mate, xc_ss.at[0, i]))
+        sends[-1].start()
+        absorb(feat, i, i == 0)
+    for i in range(parts):
+        chunk_copy(mate, i, mate, xc_ss.at[0, i]).wait_recv()
+        absorb(mate, i, False)
     for d in range(1, ny):
-        sends.append(chunk_copy(feat, ((yy + d) % ny) * 2 + cc, xy_ss.at[d]))
-        sends[-1].start()
-    sends.append(chunk_copy(feat, mate, xc_ss.at[0]))
-    sends[-1].start()
-    for d in range(ny):
-        for o in range(2):
-            q = ((yy + ny - d) % ny) * 2 + (cc if o == 0 else 1 - cc)
-            if d or o:
-                chunk_copy(q, mate, xc_ss.at[d]).wait_recv()
-            if d and not o:
-                sends.append(chunk_copy(q, mate, xc_ss.at[d]))
-                sends[-1].start()
-            xs[...] = xg[q].astype(F32).reshape(rows, width).astype(BF16)
-            if d or o:
-                gacc[...] += mm(gate[q], xs[...], NT)
-                uacc[...] += mm(lift[q], xs[...], NT)
-            else:
-                gacc[...] = mm(gate[q], xs[...], NT)
-                uacc[...] = mm(lift[q], xs[...], NT)
-    turned = (jax.nn.gelu(gacc[...], approximate=True) * uacc[...]).astype(BF16)
-    eye = jnp.where(lax.broadcasted_iota(jnp.int32, (rows, rows), 0)
-                    == lax.broadcasted_iota(jnp.int32, (rows, rows), 1), 1.0, 0.0).astype(BF16)
-    hid[...] = mm(eye, turned, NT).astype(BF16)
+        base = ahead(yy, ny - d, ny) * 2
+        for i in range(parts):
+            chunk_copy(base + cc, i, mate, xc_ss.at[d, i]).wait_recv()
+            sends.append(chunk_copy(base + cc, i, mate, xc_ss.at[d, i]))
+            sends[-1].start()
+            absorb(base + cc, i, False)
+        for i in range(parts):
+            chunk_copy(base + 1 - cc, i, mate, xc_ss.at[d, i]).wait_recv()
+            absorb(base + 1 - cc, i, False)
+    hid[...] = (jax.nn.gelu(gacc[...], approximate=True) * uacc[...]).astype(BF16)
 
     for copy in w_copies[3]:
         copy.wait()
-    total = None
+    precv_pairs = []
     for d in list(range(1, ny)) + [0]:
-        yq = (yy + d) % ny
-        core_s[d] = mm(hid[...], down[yq * 2 + (1 - cc)], NN).astype(BF16)
-        over = pltpu.make_async_remote_copy(
-            src_ref=core_s.at[d], dst_ref=core_r.at[d], send_sem=c_ss.at[d], recv_sem=c_rs.at[d],
-            device_id=(page, mate), device_id_type=MESH)
-        over.start()
-        sends.append(over)
-        part = mm(hid[...], down[yq * 2 + cc], NN)
-        over.wait_recv()
-        part = part + core_r[d].astype(F32)
-        if d:
-            y_s[d - 1] = part.astype(BF16)
-            along = pltpu.make_async_remote_copy(
-                src_ref=y_s.at[d - 1], dst_ref=y_r.at[d - 1], send_sem=y_ss.at[d - 1], recv_sem=y_rs.at[d - 1],
-                device_id=(page, yq * 2 + cc), device_id_type=MESH)
-            along.start()
-            sends.append(along)
-        else:
-            total = part
-    for d in range(1, ny):
-        pltpu.make_async_remote_copy(
-            src_ref=y_s.at[d - 1], dst_ref=y_r.at[d - 1], send_sem=y_ss.at[d - 1], recv_sem=y_rs.at[d - 1],
-            device_id=(page, mate), device_id_type=MESH).wait_recv()
-        total = total + y_r[d - 1].astype(F32)
-    psend[...] = total.reshape(n_page, BEAMS, width).astype(BF16)
-    precv[page] = psend[page]
-    p_start, p_wait, p_done = page_copy(lambda p: psend.at[p], lambda p: precv.at[p], p_ss, p_rs)
-    p_start()
-    p_wait()
+        yq = ahead(yy, d, ny)
+        over = []
+        for i, sp in enumerate(spans):
+            core_s[d, :, sp] = mm(hid[...], down[yq * 2 + (1 - cc), :, sp], NN).astype(BF16)
+            over.append(pltpu.make_async_remote_copy(
+                src_ref=core_s.at[d, :, sp], dst_ref=core_r.at[d, :, sp],
+                send_sem=c_ss.at[d, i], recv_sem=c_rs.at[d, i],
+                device_id=(page, mate), device_id_type=MESH))
+            over[i].start()
+            sends.append(over[i])
+        for i, sp in enumerate(spans):
+            part = mm(hid[...], down[yq * 2 + cc, :, sp], NN)
+            over[i].wait_recv()
+            part = part + core_r[d, :, sp].astype(F32)
+            if d:
+                y_s[d - 1, :, sp] = part.astype(BF16)
+                along = pltpu.make_async_remote_copy(
+                    src_ref=y_s.at[d - 1, :, sp], dst_ref=y_r.at[d - 1, :, sp],
+                    send_sem=y_ss.at[d - 1, i], recv_sem=y_rs.at[d - 1, i],
+                    device_id=(page, yq * 2 + cc), device_id_type=MESH)
+                along.start()
+                sends.append(along)
+                continue
+            for e in range(1, ny):
+                pltpu.make_async_remote_copy(
+                    src_ref=y_s.at[e - 1, :, sp], dst_ref=y_r.at[e - 1, :, sp],
+                    send_sem=y_ss.at[e - 1, i], recv_sem=y_rs.at[e - 1, i],
+                    device_id=(page, mate), device_id_type=MESH).wait_recv()
+                part = part + y_r[e - 1, :, sp].astype(F32)
+            psend[:, :, sp] = part.reshape(n_page, BEAMS, sp.size).astype(BF16)
+            precv[page, :, sp] = psend[page, :, sp]
+            pair = page_copy(lambda p, sp=sp: psend.at[p, :, sp], lambda p, sp=sp: precv.at[p, :, sp],
+                             p_ss.at[i], p_rs.at[i])
+            pair[0]()
+            precv_pairs.append(pair)
+    for pair in precv_pairs:
+        pair[1]()
     ff = jnp.sum(precv[...].astype(F32), axis=0)
     for g in range(n_feat):
         fsend[g] = ff[g * home:(g + 1) * home]
@@ -379,10 +411,12 @@
     st_done()
     n_done()
     lax.fori_loop(0, n_feat, lambda c, z: (pj(c)[2](), z)[1], 0)
-    ag_done()
+    for i in range(parts):
+        ag(i)[2]()
     for copy in sends:
         copy.wait_send()
-    p_done()
+    for pair in precv_pairs:
+        pair[2]()
     f_done()
 
 
@@ -407,6 +441,7 @@
         jnp.pad(g.astype(F32), (0, padded - depth)) if padded > depth else g.astype(F32)
         for g in (attention_gain, feedforward_gain, closing_gain)]).reshape(1, -1)
 
+    parts = len(halves(width))
     dma = pltpu.SemaphoreType.DMA
     scratch = [
         pltpu.VMEM(paged_keys.shape, BF16), pltpu.VMEM(paged_values.shape, BF16),
@@ -418,15 +453,14 @@
         pltpu.VMEM((sb, HEAD), F32),
         pltpu.VMEM((sb, hw), F32),
         pltpu.VMEM((sb, HEAD), F32),
-        pltpu.VMEM((n_page, BEAMS, hw + 2 * HEAD), BF16),
-        pltpu.VMEM((n_page, BEAMS, hw + 2 * HEAD), BF16),
+        pltpu.VMEM((n_page, BEAMS, hw + HEAD), BF16),
+        pltpu.VMEM((n_page, BEAMS, hw + HEAD), BF16),
         pltpu.VMEM((BEAMS, hw), BF16),
         pltpu.VMEM((n_feat, home, padded), F32),
         pltpu.VMEM((n_feat, n_feat, BEAMS, width), BF16),
         pltpu.VMEM((n_feat, BEAMS, width), F32),
         pltpu.VMEM((n_feat, n_page, BEAMS, width), BF16),
-        pltpu.VMEM((rows, width), BF16),
-        pltpu.VMEM((units, rows), F32), pltpu.VMEM((units, rows), F32),
+        pltpu.VMEM((rows, units), F32), pltpu.VMEM((rows, units), F32),
         pltpu.VMEM((rows, units), BF16),
         pltpu.VMEM((ny, rows, width), BF16), pltpu.VMEM((ny, rows, width), BF16),
         pltpu.VMEM((ny - 1, rows, width), BF16), pltpu.VMEM((ny - 1, rows, width), BF16),
@@ -437,10 +471,10 @@
         dma((n_page,)), dma((n_page,)),
         dma((n_feat,)), dma((n_feat,)),
         dma((n_feat, n_feat)), dma((n_feat, n_feat)),
-        dma((n_page,)), dma((n_page,)),
-        dma((ny,)), dma((ny,)), dma((n_feat,)),
-        dma((ny,)), dma((ny,)), dma((ny - 1,)), dma((ny - 1,)),
-        dma((n_page,)), dma((n_page,)),
+        dma((parts, n_page)), dma((parts, n_page)),
+        dma((ny, parts)), dma((ny, parts)), dma((n_feat, parts)),
+        dma((ny, parts)), dma((ny, parts)), dma((ny - 1, parts)), dma((ny - 1, parts)),
+        dma((parts, n_page)), dma((parts, n_page)),
         dma((n_feat,)), dma((n_feat,)),
     ]
     vmem = pl.BlockSpec(memory_space=pltpu.VMEM)

time: 67.8 us -> 65.9 us (0.972)
  Pallas kernels: 64.8 us -> 62.9 us
    pallas_call x1, Pallas kernels: 64.8 us -> 62.9 us  [per_device(): pl.pallas_call(functools.partial(layer_kernel, n_page, n_feat, width, dep...]
where the time goes in v4:
time: 65.9 us; the launch traced here: 65.6 us
  Pallas kernels  62.9 us (95%)
  local copies, waits for them, and re-layouts  2 us (3%)
  other arithmetic  0.74 us (1%)
    pallas_call x1, Pallas kernels, per_device(): pl.pallas_call(functools.partial(layer_kernel, n_page, n_feat, width, dep...  62.9 us
    unnamed x1, local copies, waits for them, and re-layouts  1.34 us

profile of v4, /device:TPU:0, one launch (start us, length us, event | category | flops | bytes accessed | tf_op | source)
XLA Modules:
  0.0 65.6 jit_solution(3906608627772379997)
XLA Ops:
  0.0 0.7 %maximum_convert_fusion = f32[13824]{0:T(1024)S(1)} fusion(bf16[4608]{0:T(1024)(128)(2,1)} %param.31, bf16[4608]{0:T(1024)(128)(2,1)} %param.27, bf16[4608]{0:T(1024)(128)(2,1)} %param.26), kind=kLoop, calls=%fused_computation | loop fusion | flops 82944 | bytes 82944 | tf_op jit(solution)/shard_map/reshape | solution.py:442
  0.7 0.7 %reshape.16.gains_ref = f32[1,13824]{1,0:T(1,128)} reshape(f32[13824]{0:T(1024)S(1)} %maximum_convert_fusion) | data formatting | bytes 110592 | tf_op jit(solution)/shard_map/reshape | solution.py:442
  1.4 62.9 %shard_map.154 = bf16[2,4608]{1,0:T(2,128)(2,1)} custom-call(bf16[8,1024]{1,0:T(8,128)(2,1)} %q_ref.1, bf16[8,512]{1,0:T(8,128)(2,1)} %fk_ref.1, bf16[8,512]{1,0:T(8,128)(2,1)} %fv_ref.1, s32[8,64]{1,0:T(8,128)} %bitcast.3, s32[1,64]{1,0:T(1,128)} %bitcast.4, s32[1,8]{1,0:T(1,128)} %bitcast.5, bf16[2,4608]{1,0:T(2,128)(2,1)} %stream_ref.1, ...), custom_call_target="tpu_custom_call" | custom-call | tf_op jit(solution)/shard_map/pallas_call | solution.py:482
  64.3 1.3 %copy.18 = bf16[2,4608]{1,0:T(2,128)(2,1)} copy(bf16[2,4608]{1,0:T(2,128)(2,1)} %shard_map.154) | data formatting | bytes 36864

commit v5 on v4

--- a/solution.py
+++ b/solution.py
@@ -200,66 +200,66 @@
             copy.start()
 
     half_lanes = HEAD // 2
+    pair = 2 if kv_heads % 2 == 0 else 1
+    sets = kv_heads // pair
+    ph = pair * groups
+    pw = ph * HEAD
     lane = lax.broadcasted_iota(jnp.int32, (BEAMS, HEAD), 1)
-    position = lax.broadcasted_iota(jnp.int32, (groups * BEAMS, page_len), 1).astype(F32)
-
-    def one_slot(s):
+    position = lax.broadcasted_iota(jnp.int32, (ph * BEAMS, page_len), 1).astype(F32)
+    nothing = jnp.zeros((BEAMS, HEAD), F32)
+
+    def one_slot(s, t):
         at = pl.ds(pl.multiple_of(s * BEAMS, BEAMS), BEAMS)
-        limit = jnp.concatenate([nvs[at, :]] * groups, axis=0)[:, 0:1]
-        visible = position < limit
-        sums = jnp.zeros((BEAMS, HEAD), F32)
-        for k in range(kv_heads):
-            kv = slice(k * HEAD, (k + 1) * HEAD)
-            qk = jnp.concatenate(
-                [qs[at, (k * groups + g) * HEAD:(k * groups + g + 1) * HEAD] for g in range(groups)], axis=0)
-            raw = mm(qk.astype(BF16), kbuf[s, :, kv], NT)
-            w = jnp.where(visible, capped_exp(raw), 0.0)
-            tot = jnp.sum(w, axis=1, keepdims=True)
-            num = mm(w.astype(BF16), vbuf[s, :, kv], NN)
-            for g in range(groups):
-                h = k * groups + g
-                snum[at, h * HEAD:(h + 1) * HEAD] = num[g * BEAMS:(g + 1) * BEAMS]
-                sums = jnp.where(lane % half_lanes == h, tot[g * BEAMS:(g + 1) * BEAMS], sums)
-        stot[at, :] = sums
-
-    per = 4 if slots % 4 == 0 else 1
-
-    def some_slots(i, z):
-        for u in range(per):
-            one_slot(i * per + u)
-        return z
-
-    lax.fori_loop(0, slots // per, some_slots, 0)
+        visible = position < jnp.concatenate([nvs[at, :]] * ph, axis=0)[:, 0:1]
+        qk = []
+        for i in range(ph):
+            h = t * ph + i
+            piece = qs[at, h * HEAD:(h + 1) * HEAD]
+            qk.append(jnp.concatenate([piece if j == i // groups else nothing for j in range(pair)], axis=1))
+        kv = slice(t * pair * HEAD, (t + 1) * pair * HEAD)
+        raw = mm(jnp.concatenate(qk, axis=0).astype(BF16), kbuf[s, :, kv], NT)
+        w = jnp.where(visible, capped_exp(raw), 0.0)
+        tot = jnp.sum(w, axis=1, keepdims=True)
+        num = mm(w.astype(BF16), vbuf[s, :, kv], NN)
+        sums = nothing
+        for i in range(ph):
+            h, k = t * ph + i, i // groups
+            own = slice(i * BEAMS, (i + 1) * BEAMS)
+            snum[at, h * HEAD:(h + 1) * HEAD] = num[own, k * HEAD:(k + 1) * HEAD]
+            sums = jnp.where(lane % half_lanes == i, tot[own], sums)
+        stot[t, at, :] = sums
+
+    per = 8 if slots % 8 == 0 else 1
 
     def to_rows(v):
         hi = v.astype(BF16)
         lo = (v - hi.astype(F32)).astype(BF16)
         return mm(pick, hi, TN) + mm(pick, lo, TN)
 
-    tot_rows = to_rows(stot[...])
-    tot_hi = tot_rows.astype(BF16).astype(F32)
-    first = lax.broadcasted_iota(jnp.int32, tot_rows.shape, 1) < half_lanes
-    tot_both = jnp.where(first, tot_hi, tot_rows - tot_hi)
-    nsend[:, :, 0:hw] = to_rows(snum[...]).reshape(n_page, BEAMS, hw).astype(BF16)
-    nsend[:, :, hw:hw + HEAD] = tot_both.reshape(n_page, BEAMS, HEAD).astype(BF16)
-    nrecv[page] = nsend[page]
-    n_start, n_wait, n_done = page_copy(lambda p: nsend.at[p], lambda p: nrecv.at[p], n_ss, n_rs)
-    n_start()
+    def n_copy(t):
+        return page_copy(lambda p: nsend.at[t, p], lambda p: nrecv.at[t, p], n_ss.at[t], n_rs.at[t])
+
+    for t in range(sets):
+        def some_slots(i, z, t=t):
+            for u in range(per):
+                one_slot(i * per + u, t)
+            return z
+
+        lax.fori_loop(0, slots // per, some_slots, 0)
+        tot_rows = to_rows(stot[t])
+        tot_hi = tot_rows.astype(BF16).astype(F32)
+        first = lax.broadcasted_iota(jnp.int32, tot_rows.shape, 1) < half_lanes
+        tot_both = jnp.where(first, tot_hi, tot_rows - tot_hi)
+        nsend[t, :, :, 0:pw] = to_rows(snum[:, t * pw:(t + 1) * pw]).reshape(n_page, BEAMS, pw).astype(BF16)
+        nsend[t, :, :, pw:pw + HEAD] = tot_both.reshape(n_page, BEAMS, HEAD).astype(BF16)
+        nrecv[t, page] = nsend[t, page]
+        n_copy(t)[0]()
 
     own_w = []
     for h in range(heads):
         k = h // groups
         qk = q_ref[:, h * HEAD:(h + 1) * HEAD].astype(F32) * fk_ref[:, k * HEAD:(k + 1) * HEAD].astype(F32)
         own_w.append(capped_exp(jnp.sum(qk, axis=1, keepdims=True)))
-    n_wait()
-    totals = jnp.sum(nrecv[:, :, hw:hw + HEAD].astype(F32), axis=0)
-    for h in range(heads):
-        k = h // groups
-        hs = slice(h * HEAD, (h + 1) * HEAD)
-        num = jnp.sum(nrecv[:, :, hs].astype(F32), axis=0)
-        num += own_w[h].astype(BF16).astype(F32) * fv_ref[:, k * HEAD:(k + 1) * HEAD].astype(F32)
-        att[:, hs] = (num / (totals[:, h:h + 1] + totals[:, half_lanes + h:half_lanes + h + 1] + own_w[h])).astype(BF16)
-
     for copy in w_copies[0]:
         copy.wait()
 
@@ -267,12 +267,29 @@
         return feat_copy(lambda p: prj.at[feat, c], lambda p: prj.at[p, c],
                          lambda p: pj_ss.at[p, c], lambda p: pj_rs.at[p, c])
 
-    def project(c, z):
-        prj[feat, c] = mm(att[...], wo[c], NT).astype(BF16)
-        pj(c)[0]()
-        return z
-
-    lax.fori_loop(0, n_feat, project, 0)
+    for t in range(sets):
+        n_copy(t)[1]()
+        totals = jnp.sum(nrecv[t, :, :, pw:pw + HEAD].astype(F32), axis=0)
+        for i in range(ph):
+            h = t * ph + i
+            k = h // groups
+            num = jnp.sum(nrecv[t, :, :, i * HEAD:(i + 1) * HEAD].astype(F32), axis=0)
+            num += own_w[h].astype(BF16).astype(F32) * fv_ref[:, k * HEAD:(k + 1) * HEAD].astype(F32)
+            total = totals[:, i:i + 1] + totals[:, half_lanes + i:half_lanes + i + 1] + own_w[h]
+            att[:, h * HEAD:(h + 1) * HEAD] = (num / total).astype(BF16)
+
+        def project(c, z, t=t):
+            v = mm(att[:, t * pw:(t + 1) * pw], wo[c, :, t * pw:(t + 1) * pw], NT)
+            if t:
+                v += res[c]
+            if t < sets - 1:
+                res[c] = v
+            else:
+                prj[feat, c] = v.astype(BF16)
+                pj(c)[0]()
+            return z
+
+        lax.fori_loop(0, n_feat, project, 0)
     st_wait()
     lax.fori_loop(0, n_feat, lambda c, z: (pj(c)[1](), z)[1], 0)
 
@@ -409,7 +426,8 @@
 
     q_done()
     st_done()
-    n_done()
+    for t in range(sets):
+        n_copy(t)[2]()
     lax.fori_loop(0, n_feat, lambda c, z: (pj(c)[2](), z)[1], 0)
     for i in range(parts):
         ag(i)[2]()
@@ -441,6 +459,8 @@
         jnp.pad(g.astype(F32), (0, padded - depth)) if padded > depth else g.astype(F32)
         for g in (attention_gain, feedforward_gain, closing_gain)]).reshape(1, -1)
 
+    kv_heads = kvw // HEAD
+    sets = kv_heads // 2 if kv_heads % 2 == 0 else kv_heads
     parts = len(halves(width))
     dma = pltpu.SemaphoreType.DMA
     scratch = [
@@ -452,9 +472,9 @@
         pltpu.VMEM((sb, hw), F32),
         pltpu.VMEM((sb, HEAD), F32),
         pltpu.VMEM((sb, hw), F32),
-        pltpu.VMEM((sb, HEAD), F32),
-        pltpu.VMEM((n_page, BEAMS, hw + HEAD), BF16),
-        pltpu.VMEM((n_page, BEAMS, hw + HEAD), BF16),
+        pltpu.VMEM((sets, sb, HEAD), F32),
+        pltpu.VMEM((sets, n_page, BEAMS, hw // sets + HEAD), BF16),
+        pltpu.VMEM((sets, n_page, BEAMS, hw // sets + HEAD), BF16),
         pltpu.VMEM((BEAMS, hw), BF16),
         pltpu.VMEM((n_feat, home, padded), F32),
         pltpu.VMEM((n_feat, n_feat, BEAMS, width), BF16),
@@ -468,7 +488,7 @@
         pltpu.VMEM((n_feat, home, width), F32), pltpu.VMEM((n_feat, home, width), F32),
         dma((2,)), dma((4, n_feat)),
         dma((n_page,)), dma((n_page,)),
-        dma((n_page,)), dma((n_page,)),
+        dma((sets, n_page)), dma((sets, n_page)),
         dma((n_feat,)), dma((n_feat,)),
         dma((n_feat, n_feat)), dma((n_feat, n_feat)),
         dma((parts, n_page)), dma((parts, n_page)),

time: 65.9 us -> 60.6 us (0.920)
  Pallas kernels: 62.9 us -> 57.6 us
    pallas_call x1, Pallas kernels: 62.9 us -> 57.6 us  [per_device(): pl.pallas_call(functools.partial(layer_kernel, n_page, n_feat, width, dep...]
where the time goes in v5:
time: 60.6 us; the launch traced here: 60.3 us
  Pallas kernels  57.6 us (95%)
  local copies, waits for them, and re-layouts  2 us (3%)
  other arithmetic  0.74 us (1%)
    pallas_call x1, Pallas kernels, per_device(): pl.pallas_call(functools.partial(layer_kernel, n_page, n_feat, width, dep...  57.6 us
    unnamed x1, local copies, waits for them, and re-layouts  1.34 us

profile of v5, /device:TPU:0, one launch (start us, length us, event | category | flops | bytes accessed | tf_op | source)
XLA Modules:
  0.0 60.3 jit_solution(3257381750816380144)
XLA Ops:
  0.0 0.7 %maximum_convert_fusion = f32[13824]{0:T(1024)S(1)} fusion(bf16[4608]{0:T(1024)(128)(2,1)} %param.31, bf16[4608]{0:T(1024)(128)(2,1)} %param.27, bf16[4608]{0:T(1024)(128)(2,1)} %param.26), kind=kLoop, calls=%fused_computation | loop fusion | flops 82944 | bytes 82944 | tf_op jit(solution)/shard_map/reshape | solution.py:460
  0.7 0.7 %reshape.16.gains_ref = f32[1,13824]{1,0:T(1,128)} reshape(f32[13824]{0:T(1024)S(1)} %maximum_convert_fusion) | data formatting | bytes 110592 | tf_op jit(solution)/shard_map/reshape | solution.py:460
  1.4 57.6 %shard_map.154 = bf16[2,4608]{1,0:T(2,128)(2,1)} custom-call(bf16[8,1024]{1,0:T(8,128)(2,1)} %q_ref.1, bf16[8,512]{1,0:T(8,128)(2,1)} %fk_ref.1, bf16[8,512]{1,0:T(8,128)(2,1)} %fv_ref.1, s32[8,64]{1,0:T(8,128)} %bitcast.3, s32[1,64]{1,0:T(1,128)} %bitcast.4, s32[1,8]{1,0:T(1,128)} %bitcast.5, bf16[2,4608]{1,0:T(2,128)(2,1)} %stream_ref.1, ...), custom_call_target="tpu_custom_call" | custom-call | tf_op jit(solution)/shard_map/pallas_call | solution.py:502
  59.0 1.3 %copy.18 = bf16[2,4608]{1,0:T(2,128)(2,1)} copy(bf16[2,4608]{1,0:T(2,128)(2,1)} %shard_map.154) | data formatting | bytes 36864
